TPU v7x, 32 devices: a whole 2x2x4 slice. The times are simulated.
32 devices in a mesh: row: 4 (over y, x), col: 8 (over z, core).
Axes of the slice: x: 2, y: 2, z: 4, core: 2. Of those that a mesh axis runs over, the one named last changes fastest.
Arguments:
- a_tiles: bfloat16 [3072, 3200], P(('row', 'col')), may hold values from -4 to 4
- a_owner: int32 [3072], P(('row', 'col')), may hold values from 0 to 31, as said below
- a_offset: int32 [3072, 2], P(('row', 'col')), may hold values from 0 to 560, as said below
- b_tiles: bfloat16 [3072, 3200], P(('row', 'col')), may hold values from -6 to 6
- b_owner: int32 [3072], P(('row', 'col')), may hold values from 0 to 31, as said below
- b_offset: int32 [3072, 2], P(('row', 'col')), may hold values from 0 to 560, as said below
- patch_valid: int32 [48, 128], P('row', 'col'), may hold values 0 or 1
Outputs:
- flow_field: float32 [2, 48, 128], P(None, 'row', 'col')
- mesh_field: float32 [2, 48, 128], P(None, 'row', 'col')
Inputs may be any that keep to these rules, and one draw needn't show every extreme that they name: `a_owner`: each region owner receives exactly 96 first-section tiles, one for every tile position of its region; a device sends either no tile or exactly 4 tiles to one owner. `a_offset`: row offsets are multiples of 40 below 480, column offsets multiples of 80 below 640; each owner's tiles cover its region exactly once. `b_owner`: each region owner receives exactly 96 next-section tiles, one for every tile position of its region; a device sends either no tile or exactly 4 tiles to one owner. `b_offset`: row offsets are multiples of 40 below 480, column offsets multiples of 80 below 640; each owner's tiles cover its region exactly once.
All inputs are finite; a program needn't handle non-finite values. No bound on the sum of `patch_valid` on one device may be relied on, other than what follows from the above.
Results may differ from a plain program's by a relative error of at most 0.004.
Values may be sent and summed in bfloat16 or wider, within the bound.
A program may use at most 64 MiB of HBM per device.

v0:
```python
import math

import jax
import jax.numpy as jnp
from jax import lax
from jax.sharding import PartitionSpec as P

PATCH = 160
STRIDE = 40
TY = 12
TX = 8
SWEEPS = 3
MARGIN = 60


stiffness = 1.0
tiny = 1e-06


def extended_2(block, sides, width):
    for axis, dim in sides:
        count = lax.axis_size(axis)
        forward = [(i, i + 1) for i in range(count - 1)]
        backward = [(target, source) for source, target in forward]
        low = lax.ppermute(
            lax.slice_in_dim(block, block.shape[dim] - width, None, axis=dim), axis, forward
        )
        high = lax.ppermute(lax.slice_in_dim(block, 0, width, axis=dim), axis, backward)
        block = jnp.concatenate([low, block, high], axis=dim)
    return block


def dft_tables():
    freq_index = jnp.arange(PATCH, dtype=jnp.int32)
    phase = (freq_index[:, None] * freq_index[None, :] % PATCH).astype(jnp.float32) * (
        2.0 * math.pi / PATCH
    )
    return (jnp.cos(phase).astype(jnp.bfloat16), jnp.sin(phase).astype(jnp.bfloat16))


def forward_rest(first_segment, cosine_table, sine_table):
    halves = first_segment.reshape(first_segment.shape[0], PATCH, 2, PATCH)
    left_real = jnp.stack([cosine_table, -sine_table])
    left_imag = jnp.stack([-sine_table, -cosine_table])
    spec_real = jnp.einsum("hky,nyhj->nkj", left_real, halves, preferred_element_type=jnp.float32)
    spec_imag = jnp.einsum("hky,nyhj->nkj", left_imag, halves, preferred_element_type=jnp.float32)
    return (spec_real, spec_imag)


def inverse(cross_real, cross_imag, cosine_table, sine_table):
    stacked = jnp.stack([cross_real, cross_imag], axis=2)
    right_u = jnp.stack([cosine_table, -sine_table])
    right_v = jnp.stack([sine_table, cosine_table])
    inverse_u = jnp.einsum(
        "nyhx,hxk->nyk", stacked, right_u, preferred_element_type=jnp.float32
    ).astype(jnp.bfloat16)
    inverse_v = jnp.einsum(
        "nyhx,hxk->nyk", stacked, right_v, preferred_element_type=jnp.float32
    ).astype(jnp.bfloat16)
    stacked_uv = jnp.stack([inverse_u, inverse_v], axis=2)
    left_real = jnp.stack([cosine_table, -sine_table])
    return jnp.einsum("hky,nyhj->nkj", left_real, stacked_uv, preferred_element_type=jnp.float32)


def correlate(first_a, first_b, norm_a, norm_b, cosine_table, sine_table):
    real_a, imag_a = forward_rest(first_a, cosine_table, sine_table)
    real_b, imag_b = forward_rest(first_b, cosine_table, sine_table)
    inv_norms = (1.0 / (norm_a * norm_b))[:, None, None]
    cross_real = ((real_a * real_b + imag_a * imag_b) * inv_norms).astype(jnp.bfloat16)
    cross_imag = ((real_a * imag_b - imag_a * real_b) * inv_norms).astype(jnp.bfloat16)
    correlation = inverse(cross_real, cross_imag, cosine_table, sine_table) / (PATCH * PATCH)
    weight = correlation * correlation
    weight_sum = jnp.sum(weight, axis=(1, 2))
    freq_index = jnp.arange(PATCH, dtype=jnp.int32)
    shift_units = jnp.where(freq_index < PATCH // 2, freq_index, freq_index - PATCH).astype(
        jnp.float32
    ) * (16.0 / PATCH)
    flow_y = jnp.sum(weight * shift_units[None, :, None], axis=(1, 2)) / (1.0 + weight_sum)
    flow_x = jnp.sum(weight * shift_units[None, None, :], axis=(1, 2)) / (1.0 + weight_sum)
    return (flow_y, flow_x, weight_sum / (1.0 + weight_sum))


def outgoing(tiles, tile_owner, tile_offset, slot_count, capacity, tile_h, tile_w):
    tile_count = tiles.shape[0]
    tile_index = jnp.arange(tile_count, dtype=jnp.int32)
    matches = (tile_owner[:, None] == tile_owner[None, :]) & (
        tile_index[:, None] > tile_index[None, :]
    )
    earlier_count = jnp.sum(matches.astype(jnp.int32), axis=1)
    target = tile_owner * capacity + earlier_count
    select = (jnp.arange(slot_count, dtype=jnp.int32)[:, None] == target[None, :]).astype(
        jnp.bfloat16
    )
    position = tile_offset[:, 0] // tile_h * TX + tile_offset[:, 1] // tile_w + 1
    sent_tiles = jnp.dot(select, tiles, preferred_element_type=jnp.float32).astype(jnp.bfloat16)
    slot_code = jnp.dot(
        select, position.astype(jnp.bfloat16)[:, None], preferred_element_type=jnp.float32
    ).astype(jnp.bfloat16)
    return (sent_tiles, slot_code)


def incoming(received, slot_code, tile_count, tile_h, tile_w):
    wanted = jnp.arange(1, tile_count + 1, dtype=jnp.int32).astype(jnp.float32)
    select = (slot_code[:, 0].astype(jnp.float32)[None, :] == wanted[:, None]).astype(jnp.bfloat16)
    blocks = jnp.dot(select, received, preferred_element_type=jnp.float32).astype(jnp.bfloat16)
    return (
        blocks.reshape(TY, TX, tile_h, tile_w)
        .transpose(0, 2, 1, 3)
        .reshape(TY * tile_h, TX * tile_w)
    )


def route(send_a, code_a, send_b, code_b, row_count, col_count, capacity):
    devices = row_count * col_count
    tile_size = send_a.shape[1]
    code_width = code_a.shape[1]
    recv_a, got_a, recv_b, got_b = (
        lax.all_to_all(
            send_a.reshape(devices, capacity, tile_size),
            ("row", "col"),
            split_axis=0,
            concat_axis=0,
            tiled=True,
        ),
        lax.all_to_all(
            code_a.reshape(devices, capacity, code_width),
            ("row", "col"),
            split_axis=0,
            concat_axis=0,
            tiled=True,
        ),
        lax.all_to_all(
            send_b.reshape(devices, capacity, tile_size),
            ("row", "col"),
            split_axis=0,
            concat_axis=0,
            tiled=True,
        ),
        lax.all_to_all(
            code_b.reshape(devices, capacity, code_width),
            ("row", "col"),
            split_axis=0,
            concat_axis=0,
            tiled=True,
        ),
    )
    slot_count = devices * capacity
    return (
        recv_a.reshape(slot_count, tile_size),
        got_a.reshape(slot_count, code_width),
        recv_b.reshape(slot_count, tile_size),
        got_b.reshape(slot_count, code_width),
    )


def per_device(a_tiles, a_owner, a_offset, b_tiles, b_owner, b_offset, patch_valid):
    grid_rows, grid_cols = patch_valid.shape
    tile_h = grid_rows * STRIDE // TY
    tile_w = grid_cols * STRIDE // TX
    tile_count = a_tiles.shape[0]
    row_count = lax.axis_size("row")
    col_count = lax.axis_size("col")
    devices = row_count * col_count
    capacity = 4 * tile_count // (3 * devices)
    slot_count = devices * capacity
    send_a, code_a = outgoing(a_tiles, a_owner, a_offset, slot_count, capacity, tile_h, tile_w)
    send_b, code_b = outgoing(b_tiles, b_owner, b_offset, slot_count, capacity, tile_h, tile_w)
    recv_a, got_a, recv_b, got_b = route(
        send_a, code_a, send_b, code_b, row_count, col_count, capacity
    )
    canvas_a = incoming(recv_a, got_a, tile_count, tile_h, tile_w)
    canvas_b = incoming(recv_b, got_b, tile_count, tile_h, tile_w)
    images = jnp.stack([canvas_a, canvas_b])
    padded = extended_2(images, (("row", 1), ("col", 2)), MARGIN)
    cosine_table, sine_table = dft_tables()
    column_table = jnp.concatenate([cosine_table, sine_table], axis=1).reshape(4, STRIDE, 2 * PATCH)
    cell_count = grid_cols + 3

    def one_row(grid_row):
        band_strip = lax.dynamic_slice(
            padded, (grid_row * 0, grid_row * STRIDE, grid_row * 0), (2, PATCH, cell_count * STRIDE)
        )
        cells = band_strip.reshape(2, PATCH, cell_count, STRIDE)
        first_total = jnp.zeros((2, grid_cols, PATCH, 2 * PATCH), jnp.float32)
        square_total = jnp.zeros((2, grid_cols), jnp.float32)
        for column_step in range(4):
            part_cells = cells[:, :, column_step : column_step + grid_cols, :]
            first_total = first_total + jnp.einsum(
                "ayjs,sk->ajyk",
                part_cells,
                column_table[column_step],
                preferred_element_type=jnp.float32,
            )
            values = part_cells.astype(jnp.float32)
            square_total = square_total + jnp.sum(values * values, axis=(1, 3))
        first_segment = first_total.astype(jnp.bfloat16)
        norms = PATCH * jnp.sqrt(square_total / (PATCH * PATCH) + tiny)
        return correlate(
            first_segment[0], first_segment[1], norms[0], norms[1], cosine_table, sine_table
        )

    flow_y, flow_x, confidence = lax.map(one_row, jnp.arange(grid_rows, dtype=jnp.int32))
    flow_field = jnp.stack([flow_y, flow_x])
    valid_float = patch_valid.astype(jnp.float32)
    strength = valid_float * confidence
    data_pull = strength[None] * flow_field
    initial = valid_float[None] * flow_field
    fields = jnp.concatenate(
        [strength[None], data_pull, initial, jnp.ones_like(strength)[None]], axis=0
    )
    extended = extended_2(fields, (("row", 1), ("col", 2)), SWEEPS)
    mesh_field = extended[3:5]
    for sweep_index in range(SWEEPS):
        edge = sweep_index + 1
        inner_rows = extended.shape[1] - 2 * edge
        inner_cols = extended.shape[2] - 2 * edge
        margin_fields = extended[:, edge : edge + inner_rows, edge : edge + inner_cols]
        beside_all = (
            mesh_field[:, :-2, 1:-1]
            + mesh_field[:, 2:, 1:-1]
            + mesh_field[:, 1:-1, :-2]
            + mesh_field[:, 1:-1, 2:]
        )
        mesh_field = margin_fields[5][None] * (
            (margin_fields[1:3] + stiffness * beside_all)
            / (margin_fields[0][None] + 4.0 * stiffness)
        )
    return (flow_field, mesh_field)


def solution(mesh):
    in_specs = (
        P(("row", "col"), None),
        P(("row", "col")),
        P(("row", "col"), None),
        P(("row", "col"), None),
        P(("row", "col")),
        P(("row", "col"), None),
        P("row", "col"),
    )
    out_specs = (P(None, "row", "col"), P(None, "row", "col"))
    return jax.shard_map(
        per_device, mesh=mesh, in_specs=in_specs, out_specs=out_specs, check_vma=False
    )
```

profile of v0, /device:TPU:13, one launch (start us, length us, event | category | flops | bytes accessed | tf_op | source)
XLA Modules:
  0.0 783.0 jit_solution(18131821182074934432)
XLA Ops:
  3.9 6.3 all-to-all-start.2
  15.0 4.8 all-to-all-start
  24.6 5.0 all-to-all-start.3
  31.1 18.0 %all-to-all-done.3 = bf16[32,4,3200]{2,1,0:T(4,128)(2,1)S(1)} async-done(((bf16[32,4,3200]{2,1,0:T(4,128)(2,1)}), bf16[32,4,3200]{2,1,0:T(4,128)(2,1)S(1)}, u32[]{:S(2)}, u32[]{:S(2)}) %all-to-all-start.3) | async-done | bytes 819232 | tf_op jit(solution)/shard_map/all_to_all | solution.py:132
  49.1 5.8 all-to-all-start.1
  59.3 15.1 %all-to-all-done.1 = bf16[32,4,3200]{2,1,0:T(4,128)(2,1)S(1)} async-done(((bf16[32,4,3200]{2,1,0:T(4,128)(2,1)}), bf16[32,4,3200]{2,1,0:T(4,128)(2,1)S(1)}, u32[]{:S(2)}, u32[]{:S(2)}) %all-to-all-start.1) | async-done | bytes 819232 | tf_op jit(solution)/shard_map/all_to_all | solution.py:118
  87.4 4.0 collective-permute-start.2
  95.2 4.5 collective-permute-done.3
  102.4 663.1 %while.16 = (s32[]{:T(128)}, f32[12,16]{1,0:T(8,128)S(1)}, f32[12,16]{1,0:T(8,128)S(1)}, f32[12,16]{1,0:T(8,128)}, s32[12]{0:T(128)S(1)}, /*index=5*/bf16[2,600,...) while((s32[]{:T(128)}, f32[12,16]{1,0:T(8,128)S(1)}, ...), condition=%wide.region_10.11_spmd, body=%wide.region_2.10_spmd.sunk | while | flops 2378548224 | bytes 130922496 | solution.py:202
  121.3 4.2 fusion.191
  125.5 6.4 fusion.192
  131.9 4.4 fusion.193
  136.3 3.7 copy.121
  176.5 4.2 fusion.191
  180.7 6.4 fusion.192
  187.1 4.4 fusion.193
  231.8 4.2 fusion.191
  236.0 6.4 fusion.192
  242.4 4.4 fusion.193
  287.0 4.2 fusion.191
  291.2 6.4 fusion.192
  297.6 4.4 fusion.193
  342.2 4.2 fusion.191
  346.4 6.4 fusion.192
  352.9 4.4 fusion.193
  357.3 3.7 copy.121
  397.5 4.2 fusion.191
  401.7 6.4 fusion.192
  408.1 4.4 fusion.193
  452.7 4.2 fusion.191
  456.9 6.4 fusion.192
  463.3 4.4 fusion.193
  508.0 4.2 fusion.191
  512.2 6.4 fusion.192
  518.6 4.4 fusion.193
  563.2 4.2 fusion.191
  567.4 6.4 fusion.192
  573.8 4.4 fusion.193
  618.4 4.2 fusion.191
  622.7 6.4 fusion.192
  629.1 4.4 fusion.193
  673.7 4.2 fusion.191
  677.9 6.4 fusion.192
  684.3 4.4 fusion.193
  728.9 4.2 fusion.191
  733.1 6.4 fusion.192
  739.6 4.4 fusion.193
  768.2 4.4 collective-permute-start.5
  (616 shorter events, 517.0 us)
Async XLA Ops:
  0.6 19.2 %copy-start = (bf16[96,3200]{1,0:T(8,128)(2,1)S(1)}, bf16[96,3200]{1,0:T(8,128)(2,1)}, u32[]{:S(2)}) copy-start(bf16[96,3200]{1,0:T(8,128)(2,1)} %param.12) | copy-start | bytes 1843204
  0.6 29.0 %copy-start.10 = (bf16[96,3200]{1,0:T(8,128)(2,1)S(1)}, bf16[96,3200]{1,0:T(8,128)(2,1)}, u32[]{:S(2)}) copy-start(bf16[96,3200]{1,0:T(8,128)(2,1)} %param.9) | copy-start | bytes 1843204
  3.9 11.1 %all-to-all-start.2 = ((bf16[32,4,1]{1,2,0:T(2,128)(2,1)}), bf16[32,4,1]{1,2,0:T(2,128)(2,1)S(1)}, u32[]{:S(2)}, u32[]{:S(2)}) async-start(bf16[32,4,1]{1,2,0:T(2,128)(2,1)} %reshape.265), calls=%async_computation.2 | async-start | bytes 32768 | tf_op jit(solution)/shard_map/all_to_all | solution.py:139
  15.0 9.6 %all-to-all-start = ((bf16[32,4,1]{1,2,0:T(2,128)(2,1)}), bf16[32,4,1]{1,2,0:T(2,128)(2,1)S(1)}, u32[]{:S(2)}, u32[]{:S(2)}) async-start(bf16[32,4,1]{1,2,0:T(2,128)(2,1)} %reshape.264), calls=%async_computation | async-start | bytes 32768 | tf_op jit(solution)/shard_map/all_to_all | solution.py:125
  24.6 24.5 %all-to-all-start.3 = ((bf16[32,4,3200]{2,1,0:T(4,128)(2,1)}), bf16[32,4,3200]{2,1,0:T(4,128)(2,1)S(1)}, u32[]{:S(2)}, u32[]{:S(2)}) async-start(bf16[32,4,3200]{2,1,0:T(4,128)(2,1)} %reshape.241), calls=%async_computation.3 | async-start | bytes 1638400 | tf_op jit(solution)/shard_map/all_to_all | solution.py:132
  49.1 25.3 %all-to-all-start.1 = ((bf16[32,4,3200]{2,1,0:T(4,128)(2,1)}), bf16[32,4,3200]{2,1,0:T(4,128)(2,1)S(1)}, u32[]{:S(2)}, u32[]{:S(2)}) async-start(bf16[32,4,3200]{2,1,0:T(4,128)(2,1)} %reshape.236), calls=%async_computation.1 | async-start | bytes 1638400 | tf_op jit(solution)/shard_map/all_to_all | solution.py:118
  77.0 16.3 %copy-start.11 = (bf16[4,40,160]{2,1,0:T(8,128)(2,1)S(1)}, bf16[4,40,160]{2,1,0:T(8,128)(2,1)}, u32[]{:S(2)}) copy-start(bf16[4,40,160]{2,1,0:T(8,128)(2,1)} %get-tuple-element.227) | copy-start | bytes 153604
  77.0 16.3 %copy-start.12 = (bf16[4,40,160]{2,1,0:T(8,128)(2,1)S(1)}, bf16[4,40,160]{2,1,0:T(8,128)(2,1)}, u32[]{:S(2)}) copy-start(bf16[4,40,160]{2,1,0:T(8,128)(2,1)} %get-tuple-element.228) | copy-start | bytes 153604
  77.1 16.4 %copy-start.15 = (s32[12,16]{1,0:T(8,128)S(1)}, s32[12,16]{1,0:T(8,128)}, u32[]{:S(2)}) copy-start(s32[12,16]{1,0:T(8,128)} %param.15) | copy-start | bytes 2308
  77.2 10.0 %copy-start.9 = (bf16[2,480,640]{2,1,0:T(8,128)(2,1)}, bf16[2,480,640]{2,1,0:T(8,128)(2,1)S(1)}, u32[]{:S(2)}) copy-start(bf16[2,480,640]{2,1,0:T(8,128)(2,1)S(1)} %constant_dynamic-update-slice_fusion) | copy-start | bytes 3686404
  77.3 7.6 collective-permute-start
  80.1 7.1 collective-permute-start.1
  87.4 7.7 collective-permute-start.2
  91.4 8.3 %collective-permute-start.3 = (bf16[2,600,60]{2,1,0:T(8,128)(2,1)S(1)}, bf16[2,600,60]{2,1,0:T(8,128)(2,1)}, u32[]{:S(2)}, u32[]{:S(2)}) collective-permute-start(bf16[2,600,60]{2,1,0:T(8,128)(2,1)S(1)} %get-tuple-element.210), channel_id=1, source_target_pairs={{1,0},{2,1},{3,2},{4,3},{5,4},{6,5},{7,6},{9,8},{10,9},{11,10},{12... | collective-permute-start | bytes 432008 | tf_op jit(solution)/shard_map/ppermute | solution.py:28
  102.4 663.1 %copy-start.16 = (s32[12,16]{1,0:T(8,128)S(1)}, s32[12,16]{1,0:T(8,128)}, u32[]{:S(2)}) copy-start(s32[12,16]{1,0:T(8,128)} %param.15) | copy-start | bytes 2308
  102.4 663.9 %copy-start.14 = (f32[12,16]{1,0:T(8,128)S(1)}, f32[12,16]{1,0:T(8,128)}, u32[]{:S(2)}) copy-start(f32[12,16]{1,0:T(8,128)} %convert_element_type.243) | copy-start | bytes 2308
  121.3 4.2 copy-start.3
  154.7 3.1 copy-start.8
  176.5 4.2 copy-start.3
  203.8 2.5 copy-start.5
  210.0 3.1 copy-start.8
  231.7 4.2 copy-start.3
  259.0 2.5 copy-start.5
  265.2 3.1 copy-start.8
  287.0 4.2 copy-start.3
  320.4 3.1 copy-start.8
  342.2 4.2 copy-start.3
  369.5 2.5 copy-start.5
  375.7 3.1 copy-start.8
  397.5 4.2 copy-start.3
  430.9 3.1 copy-start.8
  452.7 4.2 copy-start.3
  486.2 3.1 copy-start.8
  508.0 4.2 copy-start.3
  541.4 3.1 copy-start.8
  563.2 4.2 copy-start.3
  596.7 3.1 copy-start.8
  618.4 4.2 copy-start.3
  651.9 3.1 copy-start.8
  673.7 4.2 copy-start.3
  707.1 3.1 copy-start.8
  728.9 4.2 copy-start.3
  762.4 3.1 copy-start.8
  765.5 17.6 %copy-start.1 = (bf16[96,3200]{1,0:T(8,128)(2,1)S(1)}, bf16[96,3200]{1,0:T(8,128)(2,1)}, u32[]{:S(2)}) copy-start(bf16[96,3200]{1,0:T(8,128)(2,1)} %param.12) | copy-start | bytes 1843204
  766.3 6.3 collective-permute-start.4
  768.2 5.2 collective-permute-start.5
  773.5 5.2 collective-permute-start.6
  776.2 5.7 collective-permute-start.7
  (69 other events, 118.1 us)
where the time goes:
time: 791 us; the launch traced here: 783 us
  local copies, waits for them, and re-layouts  326 us (41%)
  matrix products  290 us (37%)
  other arithmetic  63.3 us (8%)
  waiting for transfers between devices  49.2 us (6%)
  starting transfers between devices  44.8 us (6%)
  loops' own time  8.87 us (1%)
    dot_general x48, matrix products, one_row(): jnp.einsum('ayjs,sk->ajyk', part_cells, column_table[column_step], prefer...  155 us
    while x240, local copies, waits for them, and re-layouts  130 us
    squeeze x24, local copies, waits for them, and re-layouts, forward_rest(): halves = first_segment.reshape(first_segment.shape[0], PATCH, 2, PATCH)  88.9 us
    slice x12, local copies, waits for them, and re-layouts, one_row(): first_segment[0]  53.3 us
    reduce_sum x24, other arithmetic, one_row(): square_total = square_total + jnp.sum(values * values, axis=(1, 3))  51 us
    dot_general x24, matrix products, forward_rest(): jnp.einsum('hky,nyhj->nkj', left_real, halves, preferred_element_type=jnp...  45.5 us
    dot_general x24, matrix products, forward_rest(): jnp.einsum('hky,nyhj->nkj', left_imag, halves, preferred_element_type=jnp...  38.6 us
    dot_general x12, matrix products, inverse(): jnp.einsum('hky,nyhj->nkj', left_real, stacked_uv, preferred_element_type...  20.4 us
  transfers between devices with their start and end apart: 12, of which 9 were waited for; matrix products, arithmetic and copies ran while one was open for 2% of the time, Pallas kernels for 0%

commit v1 on v0

--- a/solution.py
+++ b/solution.py
@@ -2,7 +2,11 @@
 
 import jax
 import jax.numpy as jnp
+import ml_dtypes
+import numpy as np
 from jax import lax
+from jax.experimental import pallas as pl
+from jax.experimental.pallas import tpu as pltpu
 from jax.sharding import PartitionSpec as P
 
 PATCH = 160
@@ -30,54 +34,185 @@
     return block
 
 
-def dft_tables():
-    freq_index = jnp.arange(PATCH, dtype=jnp.int32)
-    phase = (freq_index[:, None] * freq_index[None, :] % PATCH).astype(jnp.float32) * (
+HALF = PATCH // 2 + 1
+KPAD = 88
+ROWS = 608
+COLS = 768
+WIN = 208
+
+
+def tables():
+    index = np.arange(PATCH, dtype=np.int64)
+    phase = (index[:, None] * index[None, :] % PATCH).astype(np.float32) * np.float32(
         2.0 * math.pi / PATCH
     )
-    return (jnp.cos(phase).astype(jnp.bfloat16), jnp.sin(phase).astype(jnp.bfloat16))
-
-
-def forward_rest(first_segment, cosine_table, sine_table):
-    halves = first_segment.reshape(first_segment.shape[0], PATCH, 2, PATCH)
-    left_real = jnp.stack([cosine_table, -sine_table])
-    left_imag = jnp.stack([-sine_table, -cosine_table])
-    spec_real = jnp.einsum("hky,nyhj->nkj", left_real, halves, preferred_element_type=jnp.float32)
-    spec_imag = jnp.einsum("hky,nyhj->nkj", left_imag, halves, preferred_element_type=jnp.float32)
-    return (spec_real, spec_imag)
-
-
-def inverse(cross_real, cross_imag, cosine_table, sine_table):
-    stacked = jnp.stack([cross_real, cross_imag], axis=2)
-    right_u = jnp.stack([cosine_table, -sine_table])
-    right_v = jnp.stack([sine_table, cosine_table])
-    inverse_u = jnp.einsum(
-        "nyhx,hxk->nyk", stacked, right_u, preferred_element_type=jnp.float32
-    ).astype(jnp.bfloat16)
-    inverse_v = jnp.einsum(
-        "nyhx,hxk->nyk", stacked, right_v, preferred_element_type=jnp.float32
-    ).astype(jnp.bfloat16)
-    stacked_uv = jnp.stack([inverse_u, inverse_v], axis=2)
-    left_real = jnp.stack([cosine_table, -sine_table])
-    return jnp.einsum("hky,nyhj->nkj", left_real, stacked_uv, preferred_element_type=jnp.float32)
-
-
-def correlate(first_a, first_b, norm_a, norm_b, cosine_table, sine_table):
-    real_a, imag_a = forward_rest(first_a, cosine_table, sine_table)
-    real_b, imag_b = forward_rest(first_b, cosine_table, sine_table)
-    inv_norms = (1.0 / (norm_a * norm_b))[:, None, None]
-    cross_real = ((real_a * real_b + imag_a * imag_b) * inv_norms).astype(jnp.bfloat16)
-    cross_imag = ((real_a * imag_b - imag_a * real_b) * inv_norms).astype(jnp.bfloat16)
-    correlation = inverse(cross_real, cross_imag, cosine_table, sine_table) / (PATCH * PATCH)
-    weight = correlation * correlation
-    weight_sum = jnp.sum(weight, axis=(1, 2))
-    freq_index = jnp.arange(PATCH, dtype=jnp.int32)
-    shift_units = jnp.where(freq_index < PATCH // 2, freq_index, freq_index - PATCH).astype(
-        jnp.float32
-    ) * (16.0 / PATCH)
-    flow_y = jnp.sum(weight * shift_units[None, :, None], axis=(1, 2)) / (1.0 + weight_sum)
-    flow_x = jnp.sum(weight * shift_units[None, None, :], axis=(1, 2)) / (1.0 + weight_sum)
-    return (flow_y, flow_x, weight_sum / (1.0 + weight_sum))
+    cos = np.cos(phase).astype(ml_dtypes.bfloat16).astype(np.float32)
+    sin = np.sin(phase).astype(ml_dtypes.bfloat16).astype(np.float32)
+    sin[(index[:, None] * index[None, :]) % 80 == 0] = 0.0
+    first = np.zeros((2, 416, 256), np.float32)
+    for parity in range(2):
+        top = 128 + 8 * parity
+        first[parity, top : top + PATCH, :HALF] = cos[:, :HALF]
+        first[parity, top : top + PATCH, 128 : 128 + HALF] = sin[:, :HALF]
+    second = np.zeros((4 * KPAD, WIN), np.float32)
+    for parity in range(2):
+        left = STRIDE * parity
+        top = 2 * KPAD * parity
+        second[top : top + HALF, left : left + PATCH] = cos[:HALF]
+        second[top + KPAD : top + KPAD + HALF, left : left + PATCH] = sin[:HALF]
+    once = np.ones(HALF, np.float32)
+    once[0] = once[-1] = 0.5
+    third = np.zeros((PATCH, 2 * KPAD), np.float32)
+    third[:, :HALF] = cos[:, :HALF] * once
+    third[:, KPAD : KPAD + HALF] = sin[:, :HALF]
+    fourth = np.zeros((256, 256), np.float32)
+    fourth[:HALF, :PATCH] = cos[:HALF] * (2.0 * once)[:, None]
+    fourth[128 : 128 + HALF, :PATCH] = -2.0 * sin[:HALF]
+    band_rows = np.zeros((16, ROWS), np.float32)
+    for i in range(12):
+        band_rows[i, STRIDE * i : STRIDE * i + PATCH] = 1.0
+    band_cols = np.zeros((COLS, 128), np.float32)
+    for j in range(16):
+        band_cols[STRIDE * j : STRIDE * j + PATCH, j] = 1.0
+    as_bf16 = [jnp.asarray(t, jnp.bfloat16) for t in (first, second, third, fourth, band_rows)]
+    return (*as_bf16, jnp.asarray(band_cols, jnp.float32))
+
+
+def dot(left, right):
+    return jnp.dot(left, right, preferred_element_type=jnp.float32)
+
+
+def correlate_kernel(
+    images, first, second, third, fourth, band_rows, band_cols, out, spec, scale, parts
+):
+    grid_rows, grid_cols = out.shape[1], out.shape[2]
+    half_rows = ROWS // 2
+
+    def first_part(step, carry):
+        section = step // 2
+        top = pl.multiple_of(step % 2 * half_rows, 16)
+        for j in range(grid_cols):
+            left = STRIDE * j // 128 * 128
+            inside = STRIDE * j - left
+            width = 256 if inside + PATCH <= 256 else 384
+            parity = inside // 8 % 2
+            base = 128 + 8 * parity - inside
+            strip = images[section, pl.ds(top, half_rows), left : left + width]
+            spec[section, pl.ds(top, half_rows), 256 * j : 256 * (j + 1)] = dot(
+                strip, first[parity, base : base + width, :]
+            ).astype(jnp.bfloat16)
+        return carry
+
+    lax.fori_loop(0, 4, first_part, 0)
+
+    norms = []
+    for section in range(2):
+        values = images[section].astype(jnp.float32)
+        squares = values * values
+        high = squares.astype(jnp.bfloat16)
+        low = (squares - high.astype(jnp.float32)).astype(jnp.bfloat16)
+        by_rows = dot(band_rows[...], high) + dot(band_rows[...], low)
+        total = jnp.dot(
+            by_rows,
+            band_cols[...],
+            preferred_element_type=jnp.float32,
+            precision=lax.Precision.HIGHEST,
+        )
+        norms.append(PATCH * jnp.sqrt(total / (PATCH * PATCH) + tiny))
+    inv_norms = 1.0 / (norms[0] * norms[1])
+    scale[...] = (inv_norms * (1.0 / (PATCH * PATCH))) * (inv_norms * (1.0 / (PATCH * PATCH)))
+
+    lane = lax.broadcasted_iota(jnp.int32, (8, 256), 1)
+    sublane = lax.broadcasted_iota(jnp.int32, (8, 256), 0)
+    unit = 16.0 / PATCH
+    shift_x = jnp.where(lane < PATCH // 2, lane, lane - PATCH).astype(jnp.float32) * unit
+    shift_x = jnp.where(lane < PATCH, shift_x, 0.0)
+    shift_y = (sublane + PATCH // 2).astype(jnp.float32) * unit
+
+    def patch(spec_a, spec_b):
+        def combos(s):
+            a, e = s[:KPAD, :128], s[:KPAD, 128:]
+            d, b = s[KPAD:, :128], s[KPAD:, 128:]
+            return a - b, d + e, a + b, e - d
+
+        ra, ia, ra_m, ia_m = combos(spec_a)
+        rb, ib, rb_m, ib_m = combos(spec_b)
+        real, imag = ra * rb + ia * ib, ia * rb - ra * ib
+        real_m, imag_m = ra_m * rb_m + ia_m * ib_m, ia_m * rb_m - ra_m * ib_m
+        upper = jnp.concatenate([real + real_m, imag + imag_m], axis=1)
+        lower = jnp.concatenate([imag_m - imag, real - real_m], axis=1)
+        cross = jnp.concatenate([upper, lower], axis=0).astype(jnp.bfloat16)
+        inverse = dot(third[...], cross).astype(jnp.bfloat16)
+        corr = dot(inverse, fourth[...])
+        sum_0 = jnp.zeros((8, 256), jnp.float32)
+        sum_1 = jnp.zeros((8, 256), jnp.float32)
+        for block in range(PATCH // 8):
+            top = (block * 8 + PATCH // 2) % PATCH
+            piece = corr[top : top + 8]
+            sum_0 = sum_0 + piece * piece
+            sum_1 = sum_1 + sum_0
+        results = []
+        for part in (sum_0, shift_y * sum_0 - (8.0 * unit) * sum_1, shift_x * sum_0):
+            part = part[:, :128] + part[:, 128:]
+            results.append(jnp.sum(part, axis=0, keepdims=True))
+        return results
+
+    def pair_row(p, carry):
+        top = pl.multiple_of(p * (2 * STRIDE), 16)
+
+        def column(j, carry):
+            left = pl.multiple_of(j * 256, 256)
+            both = [
+                dot(second[...], spec[section, pl.ds(top, WIN), pl.ds(left, 256)])
+                for section in range(2)
+            ]
+            for parity in range(2):
+                rows = slice(2 * KPAD * parity, 2 * KPAD * (parity + 1))
+                for c, row in enumerate(patch(both[0][rows], both[1][rows])):
+                    parts[c, parity, pl.ds(j, 1), :] = row
+            return carry
+
+        lax.fori_loop(0, grid_cols, column, 0, unroll=UNROLL)
+        ones = jnp.ones((8, 128), jnp.float32)
+        for parity in range(2):
+            i = 2 * p + parity
+            sums = [
+                lax.dot_general(
+                    ones,
+                    parts[c, parity],
+                    (((1,), (1,)), ((), ())),
+                    preferred_element_type=jnp.float32,
+                    precision=lax.Precision.HIGHEST,
+                )[:1]
+                * scale[pl.ds(i, 1), :grid_cols]
+                for c in range(3)
+            ]
+            below = 1.0 + sums[0]
+            out[0, pl.ds(i, 1), :] = sums[0] / below
+            out[1, pl.ds(i, 1), :] = sums[1] / below
+            out[2, pl.ds(i, 1), :] = sums[2] / below
+        return carry
+
+    lax.fori_loop(0, grid_rows // 2, pair_row, 0)
+
+
+UNROLL = 1
+
+
+def correlate(images, grid_rows, grid_cols):
+    vmem = pl.BlockSpec(memory_space=pltpu.VMEM)
+    return pl.pallas_call(
+        correlate_kernel,
+        out_shape=jax.ShapeDtypeStruct((3, grid_rows, grid_cols), jnp.float32),
+        in_specs=[vmem] * 7,
+        out_specs=vmem,
+        scratch_shapes=[
+            pltpu.VMEM((2, ROWS, 256 * grid_cols), jnp.bfloat16),
+            pltpu.VMEM((16, 128), jnp.float32),
+            pltpu.VMEM((3, 2, grid_cols, 128), jnp.float32),
+        ],
+        compiler_params=pltpu.CompilerParams(vmem_limit_bytes=48 * 1024 * 1024),
+    )(images, *tables())
 
 
 def outgoing(tiles, tile_owner, tile_offset, slot_count, capacity, tile_h, tile_w):
@@ -172,34 +307,10 @@
     canvas_b = incoming(recv_b, got_b, tile_count, tile_h, tile_w)
     images = jnp.stack([canvas_a, canvas_b])
     padded = extended_2(images, (("row", 1), ("col", 2)), MARGIN)
-    cosine_table, sine_table = dft_tables()
-    column_table = jnp.concatenate([cosine_table, sine_table], axis=1).reshape(4, STRIDE, 2 * PATCH)
-    cell_count = grid_cols + 3
-
-    def one_row(grid_row):
-        band_strip = lax.dynamic_slice(
-            padded, (grid_row * 0, grid_row * STRIDE, grid_row * 0), (2, PATCH, cell_count * STRIDE)
-        )
-        cells = band_strip.reshape(2, PATCH, cell_count, STRIDE)
-        first_total = jnp.zeros((2, grid_cols, PATCH, 2 * PATCH), jnp.float32)
-        square_total = jnp.zeros((2, grid_cols), jnp.float32)
-        for column_step in range(4):
-            part_cells = cells[:, :, column_step : column_step + grid_cols, :]
-            first_total = first_total + jnp.einsum(
-                "ayjs,sk->ajyk",
-                part_cells,
-                column_table[column_step],
-                preferred_element_type=jnp.float32,
-            )
-            values = part_cells.astype(jnp.float32)
-            square_total = square_total + jnp.sum(values * values, axis=(1, 3))
-        first_segment = first_total.astype(jnp.bfloat16)
-        norms = PATCH * jnp.sqrt(square_total / (PATCH * PATCH) + tiny)
-        return correlate(
-            first_segment[0], first_segment[1], norms[0], norms[1], cosine_table, sine_table
-        )
-
-    flow_y, flow_x, confidence = lax.map(one_row, jnp.arange(grid_rows, dtype=jnp.int32))
+    padded = jnp.pad(
+        padded, ((0, 0), (0, ROWS - padded.shape[1]), (0, COLS - padded.shape[2]))
+    )
+    confidence, flow_y, flow_x = correlate(padded, grid_rows, grid_cols)
     flow_field = jnp.stack([flow_y, flow_x])
     valid_float = patch_valid.astype(jnp.float32)
     strength = valid_float * confidence

time: 791 us -> 189 us (0.24)
  the two profiles are of different devices: /device:TPU:13 before, /device:TPU:1 now
where the time goes in v1:
time: 189 us
  waiting for transfers between devices  68.4 us (36%)
  Pallas kernels  62.6 us (33%)
  starting transfers between devices  33.4 us (18%)
  local copies, waits for them, and re-layouts  12.9 us (7%)
  other arithmetic  5.81 us (3%)
  matrix products  4.4 us (2%)
    pallas_call x1, Pallas kernels, correlate(): pl.pallas_call(correlate_kernel, out_shape=jax.ShapeDtypeStruct((3, grid_...  62.6 us
    all_to_all x1, waiting for transfers between devices, route(): lax.all_to_all(send_a.reshape(devices, capacity, tile_size), ('row', 'col...  20.7 us
    all_to_all x1, waiting for transfers between devices, route(): lax.all_to_all(send_b.reshape(devices, capacity, tile_size), ('row', 'col...  19.2 us
    ppermute x4, waiting for transfers between devices, extended_2(): lax.ppermute(lax.slice_in_dim(block, 0, width, axis=dim), axis, backward)  15.8 us
    ppermute x4, starting transfers between devices, extended_2(): lax.ppermute(lax.slice_in_dim(block, block.shape[dim] - width, None, axis...  10.7 us
    all_to_all x1, starting transfers between devices, route(): lax.all_to_all(code_a.reshape(devices, capacity, code_width), ('row', 'co...  7.1 us
    ppermute x4, starting transfers between devices, extended_2(): lax.ppermute(lax.slice_in_dim(block, 0, width, axis=dim), axis, backward)  6.93 us
    all_to_all x1, waiting for transfers between devices, route(): lax.all_to_all(code_b.reshape(devices, capacity, code_width), ('row', 'co...  5.43 us
  transfers between devices with their start and end apart: 12, of which 10 were waited for; matrix products, arithmetic and copies ran while one was open for 5% of the time, Pallas kernels for 0%

profile of v1, /device:TPU:1, one launch (start us, length us, event | category | flops | bytes accessed | tf_op | source)
XLA Modules:
  0.0 188.6 jit_solution(845575365368228230)
XLA Ops:
  0.6 0.9 convert_reduce_fusion.1
  1.6 0.7 multiply_add_fusion.1
  2.2 0.9 fusion.15
  3.1 0.7 reshape.85
  3.9 7.1 %all-to-all-start = ((bf16[32,4,1]{1,2,0:T(2,128)(2,1)}), bf16[32,4,1]{1,2,0:T(2,128)(2,1)S(1)}, u32[]{:S(2)}, u32[]{:S(2)}) async-start(bf16[32,4,1]{1,2,0:T(2,128)(2,1)} %reshape.85), calls=%async_computation | async-start | bytes 32768 | tf_op jit(solution)/shard_map/all_to_all | solution.py:260
  11.0 0.9 convert_reduce_fusion
  11.9 0.7 multiply_add_fusion
  12.6 0.9 fusion.16
  13.5 0.7 reshape.86
  14.2 3.6 %all-to-all-done = bf16[32,4,1]{1,2,0:T(2,128)(2,1)S(1)} async-done(((bf16[32,4,1]{1,2,0:T(2,128)(2,1)}), bf16[32,4,1]{1,2,0:T(2,128)(2,1)S(1)}, u32[]{:S(2)}, u32[]{:S(2)}) %all-to-all-start) | async-done | bytes 288 | tf_op jit(solution)/shard_map/all_to_all | solution.py:260
  17.8 2.8 %all-to-all-start.2 = ((bf16[32,4,1]{1,2,0:T(2,128)(2,1)}), bf16[32,4,1]{1,2,0:T(2,128)(2,1)S(1)}, u32[]{:S(2)}, u32[]{:S(2)}) async-start(bf16[32,4,1]{1,2,0:T(2,128)(2,1)} %reshape.86), calls=%async_computation.2 | async-start | bytes 32768 | tf_op jit(solution)/shard_map/all_to_all | solution.py:274
  20.5 0.4 convolution_convert_fusion.1
  20.9 1.1 reshape.71
  22.0 5.4 %all-to-all-done.2 = bf16[32,4,1]{1,2,0:T(2,128)(2,1)S(1)} async-done(((bf16[32,4,1]{1,2,0:T(2,128)(2,1)}), bf16[32,4,1]{1,2,0:T(2,128)(2,1)S(1)}, u32[]{:S(2)}, u32[]{:S(2)}) %all-to-all-start.2) | async-done | bytes 288 | tf_op jit(solution)/shard_map/all_to_all | solution.py:274
  27.4 2.9 %all-to-all-start.1 = ((bf16[32,4,3200]{2,1,0:T(4,128)(2,1)}), bf16[32,4,3200]{2,1,0:T(4,128)(2,1)S(1)}, u32[]{:S(2)}, u32[]{:S(2)}) async-start(bf16[32,4,3200]{2,1,0:T(4,128)(2,1)} %reshape.71), calls=%async_computation.1 | async-start | bytes 1638400 | tf_op jit(solution)/shard_map/all_to_all | solution.py:253
  30.3 0.4 convolution_convert_fusion
  30.7 1.1 reshape.76
  31.8 20.7 %all-to-all-done.1 = bf16[32,4,3200]{2,1,0:T(4,128)(2,1)S(1)} async-done(((bf16[32,4,3200]{2,1,0:T(4,128)(2,1)}), bf16[32,4,3200]{2,1,0:T(4,128)(2,1)S(1)}, u32[]{:S(2)}, u32[]{:S(2)}) %all-to-all-start.1) | async-done | bytes 819232 | tf_op jit(solution)/shard_map/all_to_all | solution.py:253
  52.5 3.1 %all-to-all-start.3 = ((bf16[32,4,3200]{2,1,0:T(4,128)(2,1)}), bf16[32,4,3200]{2,1,0:T(4,128)(2,1)S(1)}, u32[]{:S(2)}, u32[]{:S(2)}) async-start(bf16[32,4,3200]{2,1,0:T(4,128)(2,1)} %reshape.76), calls=%async_computation.3 | async-start | bytes 1638400 | tf_op jit(solution)/shard_map/all_to_all | solution.py:267
  56.0 0.2 reshape.72
  56.1 0.4 convolution_convert_fusion.3
  56.5 1.1 reshape.73
  57.8 0.8 stack_reshape.6
  58.6 19.2 %all-to-all-done.3 = bf16[32,4,3200]{2,1,0:T(4,128)(2,1)S(1)} async-done(((bf16[32,4,3200]{2,1,0:T(4,128)(2,1)}), bf16[32,4,3200]{2,1,0:T(4,128)(2,1)S(1)}, u32[]{:S(2)}, u32[]{:S(2)}) %all-to-all-start.3) | async-done | bytes 819232 | tf_op jit(solution)/shard_map/all_to_all | solution.py:267
  77.8 1.1 reshape.77
  78.9 1.5 convolution_convert_fusion.2
  80.4 1.1 reshape.78
  81.5 1.1 copy.37
  82.6 2.0 %stack_reshape.7 = bf16[1,480,640]{2,1,0:T(8,128)(2,1)S(1)} reshape(bf16[12,40,8,80]{3,2,1,0:T(8,128)(2,1)} %bitcast.39) | data formatting | bytes 1228800 | tf_op jit(solution)/shard_map/stack;reshape | solution.py:308
  84.8 2.8 %collective-permute-start = (bf16[2,60,640]{2,1,0:T(8,128)(2,1)S(1)}, bf16[2,60,640]{2,1,0:T(8,128)(2,1)S(1)}, u32[]{:S(2)}, u32[]{:S(2)}) collective-permute-start(bf16[2,60,640]{2,1,0:T(8,128)(2,1)S(1)} %get-tuple-element.14), channel_id=1, source_target_pairs={{0,8},{8,16},{16,24},{1,9},{9,17},{17,25},{2,10},{10,18},{18,26},{... | collective-permute-start | bytes 460808 | tf_op jit(solution)/shard_map/ppermute | solution.py:29
  87.6 1.3 collective-permute-start.1
  88.9 2.4 %collective-permute-done = bf16[2,60,640]{2,1,0:T(8,128)(2,1)S(1)} collective-permute-done((bf16[2,60,640]{2,1,0:T(8,128)(2,1)S(1)}, bf16[2,60,640]{2,1,0:T(8,128)(2,1)S(1)}, u32[]{:S(2)}, u32[]{:S(2)}) %collective-permute-start) | collective-permute-done | bytes 153632 | tf_op jit(solution)/shard_map/ppermute | solution.py:29
  91.3 5.1 %collective-permute-done.1 = bf16[2,60,640]{2,1,0:T(8,128)(2,1)S(1)} collective-permute-done((bf16[2,60,640]{2,1,0:T(8,128)(2,1)S(1)}, bf16[2,60,640]{2,1,0:T(8,128)(2,1)S(1)}, u32[]{:S(2)}, u32[]{:S(2)}) %collective-permute-start.1) | collective-permute-done | bytes 153632 | tf_op jit(solution)/shard_map/ppermute | solution.py:32
  96.4 0.2 pad_maximum_fusion.2
  96.6 1.9 %collective-permute-start.2 = (bf16[2,600,60]{2,1,0:T(8,128)(2,1)S(1)}, bf16[2,600,60]{2,1,0:T(8,128)(2,1)S(1)}, u32[]{:S(2)}, u32[]{:S(2)}) collective-permute-start(bf16[2,600,60]{2,1,0:T(8,128)(2,1)S(1)} %get-tuple-element.12), channel_id=1, source_target_pairs={{0,1},{1,2},{2,3},{3,4},{4,5},{5,6},{6,7},{8,9},{9,10},{10,11},{11... | collective-permute-start | bytes 432008 | tf_op jit(solution)/shard_map/ppermute | solution.py:29
  98.6 2.4 %collective-permute-start.3 = (bf16[2,600,60]{2,1,0:T(8,128)(2,1)S(1)}, bf16[2,600,60]{2,1,0:T(8,128)(2,1)S(1)}, u32[]{:S(2)}, u32[]{:S(2)}) collective-permute-start(bf16[2,600,60]{2,1,0:T(8,128)(2,1)S(1)} %get-tuple-element.13), channel_id=1, source_target_pairs={{1,0},{2,1},{3,2},{4,3},{5,4},{6,5},{7,6},{9,8},{10,9},{11,10},{12... | collective-permute-start | bytes 432008 | tf_op jit(solution)/shard_map/ppermute | solution.py:32
  101.1 1.3 collective-permute-done.2
  102.3 4.4 %collective-permute-done.3 = bf16[2,600,60]{2,1,0:T(8,128)(2,1)S(1)} collective-permute-done((bf16[2,600,60]{2,1,0:T(8,128)(2,1)S(1)}, bf16[2,600,60]{2,1,0:T(8,128)(2,1)S(1)}, u32[]{:S(2)}, u32[]{:S(2)}) %collective-permute-start.3) | collective-permute-done | bytes 144032 | tf_op jit(solution)/shard_map/ppermute | solution.py:32
  106.7 1.8 fusion.8.images
  108.6 62.6 %shard_map.140 = f32[3,12,16]{2,1,0:T(8,128)S(1)} custom-call(bf16[2,608,768]{2,1,0:T(8,128)(2,1)S(1)} %fusion.8.images, bf16[2,416,256]{2,1,0:T(8,128)(2,1)S(1)} %copy-done.1, bf16[352,208]{1,0:T(8,128)(2,1)S(1)} %copy-done.3, bf16[160,176]{1,0:T(8,128)(2,1)S(1)} %copy-done.5, bf16[256,256]{1,0:T(8,128)(2,1)S(1)} %copy-done.4, ...), custom_call_target="tpu_custom_call" | custom-call | tf_op jit(solution)/shard_map/pallas_call | solution.py:204
  171.3 2.7 %collective-permute-start.4 = (f32[6,3,16]{2,1,0:T(4,128)S(1)}, f32[6,3,16]{2,1,0:T(4,128)S(1)}, u32[]{:S(2)}, u32[]{:S(2)}) collective-permute-start(f32[6,3,16]{2,1,0:T(4,128)S(1)} %get-tuple-element.22), channel_id=1, source_target_pairs={{0,8},{8,16},{16,24},{1,9},{9,17},{17,25},{2,10},{10,18},{18,26},{... | collective-permute-start | bytes 3464 | tf_op jit(solution)/shard_map/ppermute | solution.py:29
  174.0 1.3 collective-permute-start.5
  175.3 3.1 %collective-permute-done.5 = f32[6,3,16]{2,1,0:T(4,128)S(1)} collective-permute-done((f32[6,3,16]{2,1,0:T(4,128)S(1)}, f32[6,3,16]{2,1,0:T(4,128)S(1)}, u32[]{:S(2)}, u32[]{:S(2)}) %collective-permute-start.5) | collective-permute-done | bytes 1184 | tf_op jit(solution)/shard_map/ppermute | solution.py:32
  178.5 3.2 %collective-permute-start.6 = (f32[6,18,3]{2,1,0:T(8,128)S(1)}, f32[6,18,3]{2,1,0:T(8,128)S(1)}, u32[]{:S(2)}, u32[]{:S(2)}) collective-permute-start(f32[6,18,3]{2,1,0:T(8,128)S(1)} %get-tuple-element.20), channel_id=1, source_target_pairs={{0,1},{1,2},{2,3},{3,4},{4,5},{5,6},{6,7},{8,9},{9,10},{10,11},{11... | collective-permute-start | bytes 3896 | tf_op jit(solution)/shard_map/ppermute | solution.py:29
  181.8 1.9 %collective-permute-start.7 = (f32[6,18,3]{2,1,0:T(8,128)S(1)}, f32[6,18,3]{2,1,0:T(8,128)S(1)}, u32[]{:S(2)}, u32[]{:S(2)}) collective-permute-start(f32[6,18,3]{2,1,0:T(8,128)S(1)} %get-tuple-element.21), channel_id=1, source_target_pairs={{1,0},{2,1},{3,2},{4,3},{5,4},{6,5},{7,6},{9,8},{10,9},{11,10},{12... | collective-permute-start | bytes 3896 | tf_op jit(solution)/shard_map/ppermute | solution.py:32
  183.7 0.6 copy.33
  184.3 3.1 %collective-permute-done.7 = f32[6,18,3]{2,1,0:T(8,128)S(1)} collective-permute-done((f32[6,18,3]{2,1,0:T(8,128)S(1)}, f32[6,18,3]{2,1,0:T(8,128)S(1)}, u32[]{:S(2)}, u32[]{:S(2)}) %collective-permute-start.7) | collective-permute-done | bytes 1328 | tf_op jit(solution)/shard_map/ppermute | solution.py:32
  188.0 0.6 copy.34
  (42 shorter events, 1.4 us)
Async XLA Ops:
  0.6 19.9 %copy-start = (bf16[96,3200]{1,0:T(8,128)(2,1)S(1)}, bf16[96,3200]{1,0:T(8,128)(2,1)}, u32[]{:S(2)}) copy-start(bf16[96,3200]{1,0:T(8,128)(2,1)} %param.13) | copy-start | bytes 1843204
  3.9 13.9 %all-to-all-start = ((bf16[32,4,1]{1,2,0:T(2,128)(2,1)}), bf16[32,4,1]{1,2,0:T(2,128)(2,1)S(1)}, u32[]{:S(2)}, u32[]{:S(2)}) async-start(bf16[32,4,1]{1,2,0:T(2,128)(2,1)} %reshape.85), calls=%async_computation | async-start | bytes 32768 | tf_op jit(solution)/shard_map/all_to_all | solution.py:260
  17.8 9.7 %all-to-all-start.2 = ((bf16[32,4,1]{1,2,0:T(2,128)(2,1)}), bf16[32,4,1]{1,2,0:T(2,128)(2,1)S(1)}, u32[]{:S(2)}, u32[]{:S(2)}) async-start(bf16[32,4,1]{1,2,0:T(2,128)(2,1)} %reshape.86), calls=%async_computation.2 | async-start | bytes 32768 | tf_op jit(solution)/shard_map/all_to_all | solution.py:274
  20.9 9.4 %copy-start.7 = (bf16[96,3200]{1,0:T(8,128)(2,1)S(1)}, bf16[96,3200]{1,0:T(8,128)(2,1)}, u32[]{:S(2)}) copy-start(bf16[96,3200]{1,0:T(8,128)(2,1)} %param.16) | copy-start | bytes 1843204
  27.4 25.1 %all-to-all-start.1 = ((bf16[32,4,3200]{2,1,0:T(4,128)(2,1)}), bf16[32,4,3200]{2,1,0:T(4,128)(2,1)S(1)}, u32[]{:S(2)}, u32[]{:S(2)}) async-start(bf16[32,4,3200]{2,1,0:T(4,128)(2,1)} %reshape.71), calls=%async_computation.1 | async-start | bytes 1638400 | tf_op jit(solution)/shard_map/all_to_all | solution.py:253
  52.5 25.3 %all-to-all-start.3 = ((bf16[32,4,3200]{2,1,0:T(4,128)(2,1)}), bf16[32,4,3200]{2,1,0:T(4,128)(2,1)S(1)}, u32[]{:S(2)}, u32[]{:S(2)}) async-start(bf16[32,4,3200]{2,1,0:T(4,128)(2,1)} %reshape.76), calls=%async_computation.3 | async-start | bytes 1638400 | tf_op jit(solution)/shard_map/all_to_all | solution.py:267
  84.6 16.4 %copy-start.8 = (s32[12,16]{1,0:T(8,128)S(1)}, s32[12,16]{1,0:T(8,128)}, u32[]{:S(2)}) copy-start(s32[12,16]{1,0:T(8,128)} %param.19) | copy-start | bytes 2308
  84.8 6.6 %collective-permute-start = (bf16[2,60,640]{2,1,0:T(8,128)(2,1)S(1)}, bf16[2,60,640]{2,1,0:T(8,128)(2,1)S(1)}, u32[]{:S(2)}, u32[]{:S(2)}) collective-permute-start(bf16[2,60,640]{2,1,0:T(8,128)(2,1)S(1)} %get-tuple-element.14), channel_id=1, source_target_pairs={{0,8},{8,16},{16,24},{1,9},{9,17},{17,25},{2,10},{10,18},{18,26},{... | collective-permute-start | bytes 460808 | tf_op jit(solution)/shard_map/ppermute | solution.py:29
  87.6 8.8 %collective-permute-start.1 = (bf16[2,60,640]{2,1,0:T(8,128)(2,1)S(1)}, bf16[2,60,640]{2,1,0:T(8,128)(2,1)S(1)}, u32[]{:S(2)}, u32[]{:S(2)}) collective-permute-start(bf16[2,60,640]{2,1,0:T(8,128)(2,1)S(1)} %get-tuple-element.15), channel_id=1, source_target_pairs={{8,0},{16,8},{24,16},{9,1},{17,9},{25,17},{10,2},{18,10},{26,18},{... | collective-permute-start | bytes 460808 | tf_op jit(solution)/shard_map/ppermute | solution.py:32
  96.6 5.7 %collective-permute-start.2 = (bf16[2,600,60]{2,1,0:T(8,128)(2,1)S(1)}, bf16[2,600,60]{2,1,0:T(8,128)(2,1)S(1)}, u32[]{:S(2)}, u32[]{:S(2)}) collective-permute-start(bf16[2,600,60]{2,1,0:T(8,128)(2,1)S(1)} %get-tuple-element.12), channel_id=1, source_target_pairs={{0,1},{1,2},{2,3},{3,4},{4,5},{5,6},{6,7},{8,9},{9,10},{10,11},{11... | collective-permute-start | bytes 432008 | tf_op jit(solution)/shard_map/ppermute | solution.py:29
  98.6 8.2 %collective-permute-start.3 = (bf16[2,600,60]{2,1,0:T(8,128)(2,1)S(1)}, bf16[2,600,60]{2,1,0:T(8,128)(2,1)S(1)}, u32[]{:S(2)}, u32[]{:S(2)}) collective-permute-start(bf16[2,600,60]{2,1,0:T(8,128)(2,1)S(1)} %get-tuple-element.13), channel_id=1, source_target_pairs={{1,0},{2,1},{3,2},{4,3},{5,4},{6,5},{7,6},{9,8},{10,9},{11,10},{12... | collective-permute-start | bytes 432008 | tf_op jit(solution)/shard_map/ppermute | solution.py:32
  101.0 7.5 %copy-start.1 = (bf16[2,416,256]{2,1,0:T(8,128)(2,1)S(1)}, bf16[2,416,256]{2,1,0:T(8,128)(2,1)}, u32[]{:S(2)}) copy-start(bf16[2,416,256]{2,1,0:T(8,128)(2,1)} %constant.49.clone.first) | copy-start | bytes 1277956
  101.0 7.5 %copy-start.2 = (f32[768,128]{1,0:T(8,128)S(1)}, f32[768,128]{1,0:T(8,128)}, u32[]{:S(2)}) copy-start(f32[768,128]{1,0:T(8,128)} %constant.54.clone.band_cols) | copy-start | bytes 1179652
  101.0 7.5 %copy-start.3 = (bf16[352,208]{1,0:T(8,128)(2,1)S(1)}, bf16[352,208]{1,0:T(8,128)(2,1)}, u32[]{:S(2)}) copy-start(bf16[352,208]{1,0:T(8,128)(2,1)} %constant.50.clone.second) | copy-start | bytes 439300
  101.1 7.5 %copy-start.4 = (bf16[256,256]{1,0:T(8,128)(2,1)S(1)}, bf16[256,256]{1,0:T(8,128)(2,1)}, u32[]{:S(2)}) copy-start(bf16[256,256]{1,0:T(8,128)(2,1)} %constant.52.clone.fourth) | copy-start | bytes 393220
  101.1 7.5 %copy-start.5 = (bf16[160,176]{1,0:T(8,128)(2,1)S(1)}, bf16[160,176]{1,0:T(8,128)(2,1)}, u32[]{:S(2)}) copy-start(bf16[160,176]{1,0:T(8,128)(2,1)} %constant.51.clone.third) | copy-start | bytes 168964
  101.1 7.5 %copy-start.6 = (bf16[16,608]{1,0:T(8,128)(2,1)S(1)}, bf16[16,608]{1,0:T(8,128)(2,1)}, u32[]{:S(2)}) copy-start(bf16[16,608]{1,0:T(8,128)(2,1)} %constant.53.clone.band_rows) | copy-start | bytes 58372
  171.3 4.0 %collective-permute-start.4 = (f32[6,3,16]{2,1,0:T(4,128)S(1)}, f32[6,3,16]{2,1,0:T(4,128)S(1)}, u32[]{:S(2)}, u32[]{:S(2)}) collective-permute-start(f32[6,3,16]{2,1,0:T(4,128)S(1)} %get-tuple-element.22), channel_id=1, source_target_pairs={{0,8},{8,16},{16,24},{1,9},{9,17},{17,25},{2,10},{10,18},{18,26},{... | collective-permute-start | bytes 3464 | tf_op jit(solution)/shard_map/ppermute | solution.py:29
  174.0 4.4 %collective-permute-start.5 = (f32[6,3,16]{2,1,0:T(4,128)S(1)}, f32[6,3,16]{2,1,0:T(4,128)S(1)}, u32[]{:S(2)}, u32[]{:S(2)}) collective-permute-start(f32[6,3,16]{2,1,0:T(4,128)S(1)} %get-tuple-element.23), channel_id=1, source_target_pairs={{8,0},{16,8},{24,16},{9,1},{17,9},{25,17},{10,2},{18,10},{26,18},{... | collective-permute-start | bytes 3464 | tf_op jit(solution)/shard_map/ppermute | solution.py:32
  178.5 5.8 %collective-permute-start.6 = (f32[6,18,3]{2,1,0:T(8,128)S(1)}, f32[6,18,3]{2,1,0:T(8,128)S(1)}, u32[]{:S(2)}, u32[]{:S(2)}) collective-permute-start(f32[6,18,3]{2,1,0:T(8,128)S(1)} %get-tuple-element.20), channel_id=1, source_target_pairs={{0,1},{1,2},{2,3},{3,4},{4,5},{5,6},{6,7},{8,9},{9,10},{10,11},{11... | collective-permute-start | bytes 3896 | tf_op jit(solution)/shard_map/ppermute | solution.py:29
  181.8 5.7 %collective-permute-start.7 = (f32[6,18,3]{2,1,0:T(8,128)S(1)}, f32[6,18,3]{2,1,0:T(8,128)S(1)}, u32[]{:S(2)}, u32[]{:S(2)}) collective-permute-start(f32[6,18,3]{2,1,0:T(8,128)S(1)} %get-tuple-element.21), channel_id=1, source_target_pairs={{1,0},{2,1},{3,2},{4,3},{5,4},{6,5},{7,6},{9,8},{10,9},{11,10},{12... | collective-permute-start | bytes 3896 | tf_op jit(solution)/shard_map/ppermute | solution.py:32

commit v2 on v1

v2 whole, which is shorter than its diff:
```python
import math

import jax
import jax.numpy as jnp
import ml_dtypes
import numpy as np
from jax import lax
from jax.experimental import pallas as pl
from jax.experimental.pallas import tpu as pltpu
from jax.sharding import PartitionSpec as P

PATCH = 160
STRIDE = 40
TY = 12
TX = 8
SWEEPS = 3
MARGIN = 60


stiffness = 1.0
tiny = 1e-06


HALF = PATCH // 2 + 1
KPAD = 88
EDGE_R = 64
EDGE_C = 128
ROWS = 608
COLS = 896
ROW0 = EDGE_R - MARGIN
COL0 = EDGE_C - MARGIN
WIN = 208
MESH = pl.DeviceIdType.MESH


def tables():
    index = np.arange(PATCH, dtype=np.int64)
    phase = (index[:, None] * index[None, :] % PATCH).astype(np.float32) * np.float32(
        2.0 * math.pi / PATCH
    )
    cos = np.cos(phase).astype(ml_dtypes.bfloat16).astype(np.float32)
    sin = np.sin(phase).astype(ml_dtypes.bfloat16).astype(np.float32)
    sin[(index[:, None] * index[None, :]) % 80 == 0] = 0.0
    first = np.zeros((2, 416, 256), np.float32)
    for parity in range(2):
        top = 132 + 8 * parity
        first[parity, top : top + PATCH, :HALF] = cos[:, :HALF]
        first[parity, top : top + PATCH, 128 : 128 + HALF] = sin[:, :HALF]
    second = np.zeros((4 * KPAD, WIN), np.float32)
    for parity in range(2):
        left = ROW0 + STRIDE * parity
        top = 2 * KPAD * parity
        second[top : top + HALF, left : left + PATCH] = cos[:HALF]
        second[top + KPAD : top + KPAD + HALF, left : left + PATCH] = sin[:HALF]
    once = np.ones(HALF, np.float32)
    once[0] = once[-1] = 0.5
    third = np.zeros((PATCH, 2 * KPAD), np.float32)
    third[:, :HALF] = cos[:, :HALF] * once
    third[:, KPAD : KPAD + HALF] = sin[:, :HALF]
    fourth = np.zeros((256, 256), np.float32)
    fourth[:HALF, :PATCH] = cos[:HALF] * (2.0 * once)[:, None]
    fourth[128 : 128 + HALF, :PATCH] = -2.0 * sin[:HALF]
    band_rows = np.zeros((16, ROWS), np.float32)
    for i in range(12):
        band_rows[i, ROW0 + STRIDE * i : ROW0 + STRIDE * i + PATCH] = 1.0
    band_cols = np.zeros((COLS, 128), np.float32)
    for j in range(16):
        band_cols[COL0 + STRIDE * j : COL0 + STRIDE * j + PATCH, j] = 1.0
    as_bf16 = [jnp.asarray(t, jnp.bfloat16) for t in (first, second, third, fourth, band_rows)]
    return (*as_bf16, jnp.asarray(band_cols, jnp.float32))


def dot(left, right):
    return jnp.dot(left, right, preferred_element_type=jnp.float32)


def correlate_kernel(
    images, first, second, third, fourth, band_rows, band_cols, flow, sure, spec, scale, parts
):
    grid_rows, grid_cols = sure.shape
    half_rows = ROWS // 2

    def first_part(step, carry):
        section = step // 2
        top = pl.multiple_of(step % 2 * half_rows, 16)
        for j in range(grid_cols):
            left = (COL0 + STRIDE * j) // 128 * 128
            inside = COL0 + STRIDE * j - left
            width = 256 if inside + PATCH <= 256 else 384
            parity = inside // 8 % 2
            base = 132 + 8 * parity - inside
            strip = images[section, pl.ds(top, half_rows), left : left + width]
            spec[section, pl.ds(top, half_rows), 256 * j : 256 * (j + 1)] = dot(
                strip, first[parity, base : base + width, :]
            ).astype(jnp.bfloat16)
        return carry

    lax.fori_loop(0, 4, first_part, 0)

    norms = []
    for section in range(2):
        values = images[section].astype(jnp.float32)
        squares = values * values
        high = squares.astype(jnp.bfloat16)
        low = (squares - high.astype(jnp.float32)).astype(jnp.bfloat16)
        by_rows = dot(band_rows[...], high) + dot(band_rows[...], low)
        total = jnp.dot(
            by_rows,
            band_cols[...],
            preferred_element_type=jnp.float32,
            precision=lax.Precision.HIGHEST,
        )
        norms.append(PATCH * jnp.sqrt(total / (PATCH * PATCH) + tiny))
    inv_norms = 1.0 / (norms[0] * norms[1])
    scale[...] = (inv_norms * (1.0 / (PATCH * PATCH))) * (inv_norms * (1.0 / (PATCH * PATCH)))

    lane = lax.broadcasted_iota(jnp.int32, (8, 256), 1)
    sublane = lax.broadcasted_iota(jnp.int32, (8, 256), 0)
    unit = 16.0 / PATCH
    shift_x = jnp.where(lane < PATCH // 2, lane, lane - PATCH).astype(jnp.float32) * unit
    shift_x = jnp.where(lane < PATCH, shift_x, 0.0)
    shift_y = (sublane + PATCH // 2).astype(jnp.float32) * unit

    def patch(spec_a, spec_b):
        def combos(s):
            a, e = s[:KPAD, :128], s[:KPAD, 128:]
            d, b = s[KPAD:, :128], s[KPAD:, 128:]
            return a - b, d + e, a + b, e - d

        ra, ia, ra_m, ia_m = combos(spec_a)
        rb, ib, rb_m, ib_m = combos(spec_b)
        real, imag = ra * rb + ia * ib, ia * rb - ra * ib
        real_m, imag_m = ra_m * rb_m + ia_m * ib_m, ia_m * rb_m - ra_m * ib_m
        upper = jnp.concatenate([real + real_m, imag + imag_m], axis=1)
        lower = jnp.concatenate([imag_m - imag, real - real_m], axis=1)
        cross = jnp.concatenate([upper, lower], axis=0).astype(jnp.bfloat16)
        inverse = dot(third[...], cross).astype(jnp.bfloat16)
        corr = dot(inverse, fourth[...])
        sum_0 = jnp.zeros((8, 256), jnp.float32)
        sum_1 = jnp.zeros((8, 256), jnp.float32)
        for block in range(PATCH // 8):
            top = (block * 8 + PATCH // 2) % PATCH
            piece = corr[top : top + 8]
            sum_0 = sum_0 + piece * piece
            sum_1 = sum_1 + sum_0
        results = []
        for part in (sum_0, shift_y * sum_0 - (8.0 * unit) * sum_1, shift_x * sum_0):
            part = part[:, :128] + part[:, 128:]
            results.append(jnp.sum(part, axis=0, keepdims=True))
        return results

    def pair_row(p, carry):
        top = pl.multiple_of(p * (2 * STRIDE), 16)

        def column(j, carry):
            left = pl.multiple_of(j * 256, 256)
            both = [
                dot(second[...], spec[section, pl.ds(top, WIN), pl.ds(left, 256)])
                for section in range(2)
            ]
            for parity in range(2):
                rows = slice(2 * KPAD * parity, 2 * KPAD * (parity + 1))
                for c, row in enumerate(patch(both[0][rows], both[1][rows])):
                    parts[c, parity, pl.ds(j, 1), :] = row
            return carry

        lax.fori_loop(0, grid_cols, column, 0, unroll=UNROLL)
        ones = jnp.ones((8, 128), jnp.float32)
        for parity in range(2):
            i = 2 * p + parity
            sums = [
                lax.dot_general(
                    ones,
                    parts[c, parity],
                    (((1,), (1,)), ((), ())),
                    preferred_element_type=jnp.float32,
                    precision=lax.Precision.HIGHEST,
                )[:1]
                * scale[pl.ds(i, 1), :grid_cols]
                for c in range(3)
            ]
            below = 1.0 + sums[0]
            sure[pl.ds(i, 1), :] = sums[0] / below
            flow[0, pl.ds(i, 1), :] = sums[1] / below
            flow[1, pl.ds(i, 1), :] = sums[2] / below
        return carry

    lax.fori_loop(0, grid_rows // 2, pair_row, 0)


UNROLL = 2


def correlate(images, grid_rows, grid_cols):
    vmem = pl.BlockSpec(memory_space=pltpu.VMEM)
    return pl.pallas_call(
        correlate_kernel,
        out_shape=(
            jax.ShapeDtypeStruct((2, grid_rows, grid_cols), jnp.float32),
            jax.ShapeDtypeStruct((grid_rows, grid_cols), jnp.float32),
        ),
        in_specs=[vmem] * 7,
        out_specs=(vmem, vmem),
        scratch_shapes=[
            pltpu.VMEM((2, ROWS, 256 * grid_cols), jnp.bfloat16),
            pltpu.VMEM((16, 128), jnp.float32),
            pltpu.VMEM((3, 2, grid_cols, 128), jnp.float32),
        ],
        compiler_params=pltpu.CompilerParams(vmem_limit_bytes=48 * 1024 * 1024),
    )(images, *tables())


DIRECTIONS = [(dr, dc) for dr in (-1, 0, 1) for dc in (-1, 0, 1) if (dr, dc) != (0, 0)]


def exists(row, col):
    return (
        (row >= 0)
        & (row < lax.axis_size("row"))
        & (col >= 0)
        & (col < lax.axis_size("col"))
    )


def greet_neighbours(row, col):
    barrier = pltpu.get_barrier_semaphore()
    for dr, dc in DIRECTIONS:

        @pl.when(exists(row + dr, col + dc))
        def _(dr=dr, dc=dc):
            pl.semaphore_signal(
                barrier, inc=1, device_id=(row + dr, col + dc), device_id_type=MESH
            )

    def along(index, axis):
        return 1 + jnp.where(index > 0, 1, 0) + jnp.where(index < lax.axis_size(axis) - 1, 1, 0)

    pl.semaphore_wait(barrier, along(row, "row") * along(col, "col") - 1)


def exchange(row, col, copies):
    for (dr, dc), copy in zip(DIRECTIONS, copies):

        @pl.when(exists(row + dr, col + dc))
        def _(copy=copy):
            copy.start()

    for (dr, dc), copy in zip(DIRECTIONS, copies):

        @pl.when(exists(row + dr, col + dc))
        def _(copy=copy):
            copy.wait_send()

        @pl.when(exists(row - dr, col - dc))
        def _(copy=copy):
            copy.wait_recv()


def halo_kernel(canvas, image, send_sem, recv_sem):
    row, col = lax.axis_index("row"), lax.axis_index("col")
    height, width = canvas.shape[1:]
    image[:, :EDGE_R, :] = jnp.zeros((2, EDGE_R, COLS), jnp.bfloat16)
    image[:, EDGE_R + height :, :] = jnp.zeros((2, EDGE_R, COLS), jnp.bfloat16)
    side = jnp.zeros((2, height, EDGE_C), jnp.bfloat16)
    image[:, EDGE_R : EDGE_R + height, :EDGE_C] = side
    image[:, EDGE_R : EDGE_R + height, EDGE_C + width :] = side
    greet_neighbours(row, col)
    rows = {
        -1: (slice(0, EDGE_R), slice(EDGE_R + height, ROWS)),
        0: (slice(0, height), slice(EDGE_R, EDGE_R + height)),
        1: (slice(height - EDGE_R, height), slice(0, EDGE_R)),
    }
    cols = {
        -1: (slice(0, EDGE_C), slice(EDGE_C + width, COLS)),
        0: (slice(0, width), slice(EDGE_C, EDGE_C + width)),
        1: (slice(width - EDGE_C, width), slice(0, EDGE_C)),
    }
    copies = [
        pltpu.make_async_remote_copy(
            src_ref=canvas.at[:, rows[dr][0], cols[dc][0]],
            dst_ref=image.at[:, rows[dr][1], cols[dc][1]],
            send_sem=send_sem.at[d],
            recv_sem=recv_sem.at[d],
            device_id=(row + dr, col + dc),
            device_id_type=MESH,
        )
        for d, (dr, dc) in enumerate(DIRECTIONS)
    ]
    image[:, EDGE_R : EDGE_R + height, EDGE_C : EDGE_C + width] = canvas[...]
    exchange(row, col, copies)


def with_halo(canvas):
    vmem = pl.BlockSpec(memory_space=pltpu.VMEM)
    return pl.pallas_call(
        halo_kernel,
        out_shape=jax.ShapeDtypeStruct((2, ROWS, COLS), jnp.bfloat16),
        in_specs=[vmem],
        out_specs=vmem,
        scratch_shapes=[pltpu.SemaphoreType.DMA((8,)), pltpu.SemaphoreType.DMA((8,))],
        compiler_params=pltpu.CompilerParams(
            collective_id=0, has_side_effects=True, vmem_limit_bytes=32 * 1024 * 1024
        ),
    )(canvas)


def mesh_kernel(flow, sure, valid, out, mine, near, send_sem, recv_sem):
    row, col = lax.axis_index("row"), lax.axis_index("col")
    grid_rows, grid_cols = valid.shape
    near[...] = jnp.zeros(near.shape, jnp.float32)
    mine[...] = jnp.zeros(mine.shape, jnp.float32)
    usable = valid[...].astype(jnp.float32)
    mine[0, :grid_rows, :grid_cols] = usable * sure[...]
    mine[1, :grid_rows, :grid_cols] = usable * flow[0]
    mine[2, :grid_rows, :grid_cols] = usable * flow[1]
    greet_neighbours(row, col)
    copies = [
        pltpu.make_async_remote_copy(
            src_ref=mine,
            dst_ref=near.at[d],
            send_sem=send_sem.at[d],
            recv_sem=recv_sem.at[d],
            device_id=(row + dr, col + dc),
            device_id_type=MESH,
        )
        for d, (dr, dc) in enumerate(DIRECTIONS)
    ]
    exchange(row, col, copies)
    shape = mine.shape[1:]
    i = lax.broadcasted_iota(jnp.int32, shape, 0)
    j = lax.broadcasted_iota(jnp.int32, shape, 1)

    def within(index, d, count):
        low = {-1: 0, 0: SWEEPS, 1: SWEEPS + count}[d]
        high = {-1: SWEEPS, 0: SWEEPS + count, 1: 2 * SWEEPS + count}[d]
        return (index >= low) & (index < high)

    def moved(block, down, right):
        if down % shape[0]:
            block = pltpu.roll(block, down % shape[0], 0)
        if right % shape[1]:
            block = pltpu.roll(block, right % shape[1], 1)
        return block

    fields = []
    for f in range(3):
        total = jnp.zeros(shape, jnp.float32)
        for dr in (-1, 0, 1):
            for dc in (-1, 0, 1):
                if (dr, dc) == (0, 0):
                    block = mine[f]
                else:
                    block = near[DIRECTIONS.index((-dr, -dc)), f]
                block = moved(block, SWEEPS + grid_rows * dr, SWEEPS + grid_cols * dc)
                here = within(i, dr, grid_rows) & within(j, dc, grid_cols)
                total = jnp.where(here, block, total)
        fields.append(total)
    strength, start_y, start_x = fields
    grid_i = row * grid_rows + i - SWEEPS
    grid_j = col * grid_cols + j - SWEEPS
    inside = (
        (grid_i >= 0)
        & (grid_i < lax.axis_size("row") * grid_rows)
        & (grid_j >= 0)
        & (grid_j < lax.axis_size("col") * grid_cols)
        & (i < grid_rows + 2 * SWEEPS)
        & (j < grid_cols + 2 * SWEEPS)
    )
    for f, start in enumerate((start_y, start_x)):
        pull = strength * start
        field = start
        for _ in range(SWEEPS):
            around = moved(field, 1, 0) + moved(field, -1, 0)
            around = around + moved(field, 0, 1) + moved(field, 0, -1)
            field = (pull + stiffness * around) / (strength + 4.0 * stiffness)
            field = jnp.where(inside, field, 0.0)
        out[f] = moved(field, -SWEEPS, -SWEEPS)[:grid_rows, :grid_cols]


def relaxed(flow, sure, valid):
    vmem = pl.BlockSpec(memory_space=pltpu.VMEM)
    return pl.pallas_call(
        mesh_kernel,
        out_shape=jax.ShapeDtypeStruct(flow.shape, jnp.float32),
        in_specs=[vmem] * 3,
        out_specs=vmem,
        scratch_shapes=[
            pltpu.VMEM((3, 24, 128), jnp.float32),
            pltpu.VMEM((8, 3, 24, 128), jnp.float32),
            pltpu.SemaphoreType.DMA((8,)),
            pltpu.SemaphoreType.DMA((8,)),
        ],
        compiler_params=pltpu.CompilerParams(collective_id=1, has_side_effects=True),
    )(flow, sure, valid)


def slots(tile_owner):
    index = jnp.arange(tile_owner.shape[0], dtype=jnp.int32)
    earlier = (tile_owner[:, None] == tile_owner[None, :]) & (index[:, None] > index[None, :])
    return tile_owner, jnp.sum(earlier.astype(jnp.int32), axis=1)


def routed(tiles, owners, offsets, devices, capacity, tile_h, tile_w):
    tile_count, tile_size = tiles[0].shape
    targets, rows = [], []
    for section in range(2):
        owner, rank = slots(owners[section])
        targets.append(owner * (2 * capacity) + section * capacity + rank)
        offset = offsets[section]
        place = offset[:, 0] // tile_h * TX + offset[:, 1] // tile_w + 1
        code = jnp.pad(place.astype(jnp.bfloat16)[:, None], ((0, 0), (0, 127)))
        rows.append(jnp.concatenate([tiles[section], code], axis=1))
    target = jnp.concatenate(targets)
    slot = jnp.arange(devices * 2 * capacity, dtype=jnp.int32)
    select = (slot[:, None] == target[None, :]).astype(jnp.bfloat16)
    sent = jnp.dot(
        select, jnp.concatenate(rows, axis=0), preferred_element_type=jnp.float32
    ).astype(jnp.bfloat16)
    got = lax.all_to_all(
        sent.reshape(devices, 2 * capacity, tile_size + 128),
        ("row", "col"),
        split_axis=0,
        concat_axis=0,
        tiled=True,
    ).reshape(devices * 2 * capacity, tile_size + 128)
    came = slot // capacity % 2 * tile_count + got[:, tile_size].astype(jnp.int32) - 1
    came = jnp.where(got[:, tile_size] > 0, came, -1)
    wanted = jnp.arange(2 * tile_count, dtype=jnp.int32)
    select = (came[None, :] == wanted[:, None]).astype(jnp.bfloat16)
    blocks = jnp.dot(
        select, got[:, :tile_size], preferred_element_type=jnp.float32
    ).astype(jnp.bfloat16)
    return (
        blocks.reshape(2, TY, TX, tile_h, tile_w)
        .transpose(0, 1, 3, 2, 4)
        .reshape(2, TY * tile_h, TX * tile_w)
    )


def per_device(a_tiles, a_owner, a_offset, b_tiles, b_owner, b_offset, patch_valid):
    grid_rows, grid_cols = patch_valid.shape
    tile_h = grid_rows * STRIDE // TY
    tile_w = grid_cols * STRIDE // TX
    devices = lax.axis_size("row") * lax.axis_size("col")
    capacity = 4 * a_tiles.shape[0] // (3 * devices)
    canvas = routed(
        (a_tiles, b_tiles),
        (a_owner, b_owner),
        (a_offset, b_offset),
        devices,
        capacity,
        tile_h,
        tile_w,
    )
    flow_field, confidence = correlate(with_halo(canvas), grid_rows, grid_cols)
    return flow_field, relaxed(flow_field, confidence, patch_valid)


def solution(mesh):
    in_specs = (
        P(("row", "col"), None),
        P(("row", "col")),
        P(("row", "col"), None),
        P(("row", "col"), None),
        P(("row", "col")),
        P(("row", "col"), None),
        P("row", "col"),
    )
    out_specs = (P(None, "row", "col"), P(None, "row", "col"))
    return jax.shard_map(
        per_device, mesh=mesh, in_specs=in_specs, out_specs=out_specs, check_vma=False
    )
```

time: 189 us -> 142 us (0.75)
  the two profiles are of different devices: /device:TPU:1 before, /device:TPU:13 now
where the time goes in v2:
time: 142 us; the launch traced here: 141 us
  Pallas kernels  78.9 us (56%)
  blocking collectives  44.8 us (32%)
  local copies, waits for them, and re-layouts  9.94 us (7%)
  other arithmetic  4.38 us (3%)
  matrix products  2.36 us (2%)
    pallas_call x1, Pallas kernels, correlate(): pl.pallas_call(correlate_kernel, out_shape=(jax.ShapeDtypeStruct((2, grid...  54.1 us
    all_to_all x1, blocking collectives, routed(): lax.all_to_all(sent.reshape(devices, 2 * capacity, tile_size + 128), ('ro...  44.8 us
    pallas_call x1, Pallas kernels, with_halo(): pl.pallas_call(halo_kernel, out_shape=jax.ShapeDtypeStruct((2, ROWS, COLS...  14.2 us
    pallas_call x1, Pallas kernels, relaxed(): pl.pallas_call(mesh_kernel, out_shape=jax.ShapeDtypeStruct(flow.shape, jn...  10.6 us
    reshape x2, local copies, waits for them, and re-layouts, routed(): blocks.reshape(2, TY, TX, tile_h, tile_w).transpose(0, 1, 3, 2, 4)  3.86 us
    reshape x1, local copies, waits for them, and re-layouts, routed(): return blocks.reshape(2, TY, TX, tile_h, tile_w).transpose(0, 1, 3, 2, 4)...  3.24 us

profile of v2, /device:TPU:13, one launch (start us, length us, event | category | flops | bytes accessed | tf_op | source)
XLA Modules:
  0.0 141.2 jit_solution(15703735045545812341)
XLA Ops:
  0.6 0.8 add_convert_fusion.1
  1.4 0.8 add_convert_fusion
  2.2 0.9 convert_reduce_fusion.2
  3.1 0.9 convert_reduce_fusion.1
  4.0 0.1 copy.37
  4.1 0.1 copy.36
  4.3 0.7 add_add_fusion
  5.0 0.1 pad_add_fusion
  5.0 1.9 %fusion = bf16[32,8,3328]{2,1,0:T(8,128)(2,1)S(1)} fusion(bf16[96,1]{1,0:T(8,128)(2,1)S(1)} %copy.37, bf16[96,1]{1,0:T(8,128)(2,1)S(1)} %copy.36, bf16[96,3200]{1,0:T(8,128)(2,1)} %param.16, bf16[96,3200]{1,0:T(8,128)(2,1)} %param.13, s32[192]{0:T(256)S(1)} %pad_add_fusion), kind=kOutput, calls=%fused_computation.2 | convolution fusion | flops 338919424 | bytes 2933888 | tf_op jit(solution)/shard_map/dot_general | solution.py:416
  6.9 44.8 %all_to_all.5 = bf16[32,8,3328]{2,1,0:T(8,128)(2,1)S(1)} all-to-all(bf16[32,8,3328]{2,1,0:T(8,128)(2,1)S(1)} %fusion), channel_id=1, replica_groups=mesh['row'=4,'col'=8] {'row','col'}, dimensions={0} | all-to-all | bytes 3407872 | tf_op jit(solution)/shard_map/all_to_all | solution.py:419
  51.7 0.1 compare_reduce_fusion
  51.8 0.1 convert_reduce_fusion
  51.9 0.5 convolution_convert_fusion.1
  52.4 2.2 %reshape.64 = bf16[2,12,8,40,80]{4,3,2,1,0:T(8,128)(2,1)S(1)} reshape(bf16[192,3200]{1,0:T(8,128)(2,1)S(1)} %convolution_convert_fusion.1) | data formatting | bytes 2457600 | tf_op jit(solution)/shard_map/reshape | solution.py:434
  54.6 1.7 %copy.39 = bf16[2,12,8,40,80]{4,2,3,1,0:T(8,128)(2,1)} copy(bf16[2,12,8,40,80]{4,3,2,1,0:T(8,128)(2,1)S(1)} %reshape.64) | data formatting | bytes 2457600 | tf_op jit(solution)/shard_map/reshape | solution.py:434
  56.3 3.2 %reshape.65.canvas = bf16[2,480,640]{2,1,0:T(8,128)(2,1)S(1)} reshape(bf16[2,12,40,8,80]{4,3,2,1,0:T(8,128)(2,1)} %bitcast.8) | data formatting | bytes 2457600 | tf_op jit(solution)/shard_map/reshape | solution.py:436
  59.6 0.0 copy-start
  59.6 0.0 copy-start.1
  59.6 0.0 copy-start.2
  59.6 0.0 copy-start.3
  59.6 0.0 copy-start.4
  59.6 0.0 copy-start.6
  59.6 14.2 %shard_map.140.images = bf16[2,608,896]{2,1,0:T(8,128)(2,1)S(1)} custom-call(bf16[2,480,640]{2,1,0:T(8,128)(2,1)S(1)} %reshape.65.canvas), custom_call_target="tpu_custom_call" | custom-call | tf_op jit(solution)/shard_map/pallas_call | solution.py:295
  73.8 0.0 copy-done
  73.8 0.0 copy-done.1
  73.8 0.0 copy-done.2
  73.9 0.0 copy-done.3
  73.9 0.0 copy-done.4
  73.9 0.0 copy-done.6
  73.9 54.1 %shard_map.141 = (f32[2,12,16]{2,1,0:T(8,128)S(1)}, f32[12,16]{1,0:T(8,128)S(1)}) custom-call(bf16[2,608,896]{2,1,0:T(8,128)(2,1)S(1)} %shard_map.140.images, bf16[2,416,256]{2,1,0:T(8,128)(2,1)S(1)} %copy-done.1, bf16[352,208]{1,0:T(8,128)(2,1)S(1)} %copy-done.2, bf16[160,176]{1,0:T(8,128)(2,1)S(1)} %copy-done.4, bf16[256,256]{1,0:T(8,128)(2,1)S(1)} %copy-done.3, ...), custom_call_target="tpu_custom_call" | custom-call | tf_op jit(solution)/shard_map/pallas_call | solution.py:196
  128.0 0.0 copy-start.7
  128.0 0.6 copy-done.7
  128.6 0.0 copy-start.5
  128.6 0.6 copy.34
  129.2 0.0 copy-done.5
  129.2 10.6 %shard_map.142 = f32[2,12,16]{2,1,0:T(8,128)} custom-call(f32[2,12,16]{2,1,0:T(8,128)} %copy-done.5, f32[12,16]{1,0:T(8,128)} %copy-done.7, s32[12,16]{1,0:T(8,128)} %valid.1), custom_call_target="tpu_custom_call" | custom-call | tf_op jit(solution)/shard_map/pallas_call | solution.py:382
  139.9 1.3 copy.35
  (1 shorter events, 0.0 us)
Async XLA Ops:
  59.6 14.3 %copy-start = (f32[896,128]{1,0:T(8,128)S(1)}, f32[896,128]{1,0:T(8,128)}, u32[]{:S(2)}) copy-start(f32[896,128]{1,0:T(8,128)} %constant.81.clone.band_cols) | copy-start | bytes 1376260
  59.6 14.3 %copy-start.1 = (bf16[2,416,256]{2,1,0:T(8,128)(2,1)S(1)}, bf16[2,416,256]{2,1,0:T(8,128)(2,1)}, u32[]{:S(2)}) copy-start(bf16[2,416,256]{2,1,0:T(8,128)(2,1)} %constant.76.clone.first) | copy-start | bytes 1277956
  59.6 14.3 %copy-start.2 = (bf16[352,208]{1,0:T(8,128)(2,1)S(1)}, bf16[352,208]{1,0:T(8,128)(2,1)}, u32[]{:S(2)}) copy-start(bf16[352,208]{1,0:T(8,128)(2,1)} %constant.77.clone.second) | copy-start | bytes 439300
  59.6 14.3 %copy-start.3 = (bf16[256,256]{1,0:T(8,128)(2,1)S(1)}, bf16[256,256]{1,0:T(8,128)(2,1)}, u32[]{:S(2)}) copy-start(bf16[256,256]{1,0:T(8,128)(2,1)} %constant.79.clone.fourth) | copy-start | bytes 393220
  59.6 14.3 %copy-start.4 = (bf16[160,176]{1,0:T(8,128)(2,1)S(1)}, bf16[160,176]{1,0:T(8,128)(2,1)}, u32[]{:S(2)}) copy-start(bf16[160,176]{1,0:T(8,128)(2,1)} %constant.78.clone.third) | copy-start | bytes 168964
  59.6 14.2 %copy-start.6 = (bf16[16,608]{1,0:T(8,128)(2,1)S(1)}, bf16[16,608]{1,0:T(8,128)(2,1)}, u32[]{:S(2)}) copy-start(bf16[16,608]{1,0:T(8,128)(2,1)} %constant.80.clone.band_rows) | copy-start | bytes 58372
  128.0 0.6 copy-start.7
  128.6 0.6 copy-start.5

commit v3 on v2

--- a/solution.py
+++ b/solution.py
@@ -75,7 +75,8 @@
 
 
 def correlate_kernel(
-    images, first, second, third, fourth, band_rows, band_cols, flow, sure, spec, scale, parts
+    images, first, second, third, fourth, band_rows, band_cols, flow, sure, spec, scale, parts,
+    spectra_0, spectra_1, inverse_0, inverse_1,
 ):
     grid_rows, grid_cols = sure.shape
     half_rows = ROWS // 2
@@ -121,74 +122,85 @@
     shift_x = jnp.where(lane < PATCH, shift_x, 0.0)
     shift_y = (sublane + PATCH // 2).astype(jnp.float32) * unit
 
-    def patch(spec_a, spec_b):
-        def combos(s):
-            a, e = s[:KPAD, :128], s[:KPAD, 128:]
-            d, b = s[KPAD:, :128], s[KPAD:, 128:]
-            return a - b, d + e, a + b, e - d
-
-        ra, ia, ra_m, ia_m = combos(spec_a)
-        rb, ib, rb_m, ib_m = combos(spec_b)
-        real, imag = ra * rb + ia * ib, ia * rb - ra * ib
-        real_m, imag_m = ra_m * rb_m + ia_m * ib_m, ia_m * rb_m - ra_m * ib_m
-        upper = jnp.concatenate([real + real_m, imag + imag_m], axis=1)
-        lower = jnp.concatenate([imag_m - imag, real - real_m], axis=1)
-        cross = jnp.concatenate([upper, lower], axis=0).astype(jnp.bfloat16)
-        inverse = dot(third[...], cross).astype(jnp.bfloat16)
-        corr = dot(inverse, fourth[...])
-        sum_0 = jnp.zeros((8, 256), jnp.float32)
-        sum_1 = jnp.zeros((8, 256), jnp.float32)
-        for block in range(PATCH // 8):
-            top = (block * 8 + PATCH // 2) % PATCH
-            piece = corr[top : top + 8]
-            sum_0 = sum_0 + piece * piece
-            sum_1 = sum_1 + sum_0
-        results = []
-        for part in (sum_0, shift_y * sum_0 - (8.0 * unit) * sum_1, shift_x * sum_0):
-            part = part[:, :128] + part[:, 128:]
-            results.append(jnp.sum(part, axis=0, keepdims=True))
-        return results
-
-    def pair_row(p, carry):
-        top = pl.multiple_of(p * (2 * STRIDE), 16)
-
-        def column(j, carry):
-            left = pl.multiple_of(j * 256, 256)
-            both = [
-                dot(second[...], spec[section, pl.ds(top, WIN), pl.ds(left, 256)])
-                for section in range(2)
-            ]
-            for parity in range(2):
-                rows = slice(2 * KPAD * parity, 2 * KPAD * (parity + 1))
-                for c, row in enumerate(patch(both[0][rows], both[1][rows])):
-                    parts[c, parity, pl.ds(j, 1), :] = row
-            return carry
-
-        lax.fori_loop(0, grid_cols, column, 0, unroll=UNROLL)
-        ones = jnp.ones((8, 128), jnp.float32)
+    pairs = grid_rows // 2 * grid_cols
+
+    def forward(t, spectra):
+        t = jnp.minimum(t, pairs - 1)
+        top = pl.multiple_of(t // grid_cols * (2 * STRIDE), 16)
+        left = pl.multiple_of(t % grid_cols * 256, 256)
+        for section in range(2):
+            spectra[section] = dot(second[...], spec[section, pl.ds(top, WIN), pl.ds(left, 256)])
+
+    def combos(spectra, section, parity):
+        top = 2 * KPAD * parity
+        a = spectra[section, top : top + KPAD, :128]
+        e = spectra[section, top : top + KPAD, 128:]
+        d = spectra[section, top + KPAD : top + 2 * KPAD, :128]
+        b = spectra[section, top + KPAD : top + 2 * KPAD, 128:]
+        return a - b, d + e, a + b, e - d
+
+    def crossed(spectra, inverse):
         for parity in range(2):
-            i = 2 * p + parity
-            sums = [
-                lax.dot_general(
-                    ones,
-                    parts[c, parity],
-                    (((1,), (1,)), ((), ())),
-                    preferred_element_type=jnp.float32,
-                    precision=lax.Precision.HIGHEST,
-                )[:1]
-                * scale[pl.ds(i, 1), :grid_cols]
-                for c in range(3)
-            ]
-            below = 1.0 + sums[0]
-            sure[pl.ds(i, 1), :] = sums[0] / below
-            flow[0, pl.ds(i, 1), :] = sums[1] / below
-            flow[1, pl.ds(i, 1), :] = sums[2] / below
+            ra, ia, ra_m, ia_m = combos(spectra, 0, parity)
+            rb, ib, rb_m, ib_m = combos(spectra, 1, parity)
+            real, imag = ra * rb + ia * ib, ia * rb - ra * ib
+            real_m, imag_m = ra_m * rb_m + ia_m * ib_m, ia_m * rb_m - ra_m * ib_m
+            upper = jnp.concatenate([real + real_m, imag + imag_m], axis=1)
+            lower = jnp.concatenate([imag_m - imag, real - real_m], axis=1)
+            cross = jnp.concatenate([upper, lower], axis=0).astype(jnp.bfloat16)
+            inverse[PATCH * parity : PATCH * (parity + 1)] = dot(third[...], cross).astype(
+                jnp.bfloat16
+            )
+
+    def summed(t, inverse):
+        corr = dot(inverse[...], fourth[...])
+        for parity in range(2):
+            sum_0 = jnp.zeros((8, 256), jnp.float32)
+            sum_1 = jnp.zeros((8, 256), jnp.float32)
+            for block in range(PATCH // 8):
+                top = PATCH * parity + (block * 8 + PATCH // 2) % PATCH
+                piece = corr[top : top + 8]
+                sum_0 = sum_0 + piece * piece
+                sum_1 = sum_1 + sum_0
+            moments = (sum_0, shift_y * sum_0 - (8.0 * unit) * sum_1, shift_x * sum_0)
+            for c, part in enumerate(moments):
+                part = part[:, :128] + part[:, 128:]
+                parts[c, parity, pl.ds(t + 1, 1), :] = jnp.sum(part, axis=0, keepdims=True)
+
+    inverse_1[...] = jnp.zeros(inverse_1.shape, jnp.bfloat16)
+    forward(0, spectra_0)
+
+    def step(u, carry):
+        t = 2 * u
+        summed(t - 1, inverse_1)
+        crossed(spectra_0, inverse_0)
+        forward(t + 1, spectra_1)
+        summed(t, inverse_0)
+        crossed(spectra_1, inverse_1)
+        forward(t + 2, spectra_0)
         return carry
 
-    lax.fori_loop(0, grid_rows // 2, pair_row, 0)
-
-
-UNROLL = 2
+    lax.fori_loop(0, pairs // 2, step, 0)
+    summed(pairs - 1, inverse_1)
+
+    ones = jnp.ones((8, 128), jnp.float32)
+    for i in range(grid_rows):
+        first_pair = i // 2 * grid_cols + 1
+        sums = [
+            lax.dot_general(
+                ones,
+                parts[c, i % 2, first_pair : first_pair + grid_cols, :],
+                (((1,), (1,)), ((), ())),
+                preferred_element_type=jnp.float32,
+                precision=lax.Precision.HIGHEST,
+            )[:1]
+            * scale[i : i + 1, :grid_cols]
+            for c in range(3)
+        ]
+        below = 1.0 + sums[0]
+        sure[i : i + 1, :] = sums[0] / below
+        flow[0, i : i + 1, :] = sums[1] / below
+        flow[1, i : i + 1, :] = sums[2] / below
 
 
 def correlate(images, grid_rows, grid_cols):
@@ -204,7 +216,11 @@
         scratch_shapes=[
             pltpu.VMEM((2, ROWS, 256 * grid_cols), jnp.bfloat16),
             pltpu.VMEM((16, 128), jnp.float32),
-            pltpu.VMEM((3, 2, grid_cols, 128), jnp.float32),
+            pltpu.VMEM((3, 2, grid_rows // 2 * grid_cols + 8, 128), jnp.float32),
+            pltpu.VMEM((2, 4 * KPAD, 256), jnp.float32),
+            pltpu.VMEM((2, 4 * KPAD, 256), jnp.float32),
+            pltpu.VMEM((2 * PATCH, 256), jnp.bfloat16),
+            pltpu.VMEM((2 * PATCH, 256), jnp.bfloat16),
         ],
         compiler_params=pltpu.CompilerParams(vmem_limit_bytes=48 * 1024 * 1024),
     )(images, *tables())

time: 142 us -> 125 us (0.88)
  Pallas kernels: 78.9 us -> 62.2 us
    pallas_call x1, Pallas kernels: 54.1 us -> 37.3 us  [correlate(): pl.pallas_call(correlate_kernel, out_shape=(jax.ShapeDtypeStruct((2, grid...]
where the time goes in v3:
time: 125 us; the launch traced here: 124 us
  Pallas kernels  62.2 us (50%)
  blocking collectives  44.8 us (36%)
  local copies, waits for them, and re-layouts  9.95 us (8%)
  other arithmetic  4.38 us (4%)
  matrix products  2.36 us (2%)
    all_to_all x1, blocking collectives, routed(): lax.all_to_all(sent.reshape(devices, 2 * capacity, tile_size + 128), ('ro...  44.8 us
    pallas_call x1, Pallas kernels, correlate(): pl.pallas_call(correlate_kernel, out_shape=(jax.ShapeDtypeStruct((2, grid...  37.3 us
    pallas_call x1, Pallas kernels, with_halo(): pl.pallas_call(halo_kernel, out_shape=jax.ShapeDtypeStruct((2, ROWS, COLS...  14.2 us
    pallas_call x1, Pallas kernels, relaxed(): pl.pallas_call(mesh_kernel, out_shape=jax.ShapeDtypeStruct(flow.shape, jn...  10.7 us
    reshape x2, local copies, waits for them, and re-layouts, routed(): blocks.reshape(2, TY, TX, tile_h, tile_w).transpose(0, 1, 3, 2, 4)  3.86 us
    reshape x1, local copies, waits for them, and re-layouts, routed(): return blocks.reshape(2, TY, TX, tile_h, tile_w).transpose(0, 1, 3, 2, 4)...  3.24 us
    unnamed x20, local copies, waits for them, and re-layouts  2.85 us

profile of v3, /device:TPU:13, one launch (start us, length us, event | category | flops | bytes accessed | tf_op | source)
XLA Modules:
  0.0 124.4 jit_solution(7699130476886512410)
XLA Ops:
  0.6 0.8 add_convert_fusion.1
  1.4 0.8 add_convert_fusion
  2.2 0.9 convert_reduce_fusion.2
  3.1 0.9 convert_reduce_fusion.1
  4.0 0.1 copy.37
  4.1 0.1 copy.36
  4.3 0.7 add_add_fusion
  5.0 0.1 pad_add_fusion
  5.0 1.9 %fusion = bf16[32,8,3328]{2,1,0:T(8,128)(2,1)S(1)} fusion(bf16[96,1]{1,0:T(8,128)(2,1)S(1)} %copy.37, bf16[96,1]{1,0:T(8,128)(2,1)S(1)} %copy.36, bf16[96,3200]{1,0:T(8,128)(2,1)} %param.16, bf16[96,3200]{1,0:T(8,128)(2,1)} %param.13, s32[192]{0:T(256)S(1)} %pad_add_fusion), kind=kOutput, calls=%fused_computation.2 | convolution fusion | flops 338919424 | bytes 2933888 | tf_op jit(solution)/shard_map/dot_general | solution.py:432
  6.9 44.8 %all_to_all.5 = bf16[32,8,3328]{2,1,0:T(8,128)(2,1)S(1)} all-to-all(bf16[32,8,3328]{2,1,0:T(8,128)(2,1)S(1)} %fusion), channel_id=1, replica_groups=mesh['row'=4,'col'=8] {'row','col'}, dimensions={0} | all-to-all | bytes 3407872 | tf_op jit(solution)/shard_map/all_to_all | solution.py:435
  51.7 0.1 compare_reduce_fusion
  51.8 0.1 convert_reduce_fusion
  51.9 0.5 convolution_convert_fusion.1
  52.4 2.2 %reshape.64 = bf16[2,12,8,40,80]{4,3,2,1,0:T(8,128)(2,1)S(1)} reshape(bf16[192,3200]{1,0:T(8,128)(2,1)S(1)} %convolution_convert_fusion.1) | data formatting | bytes 2457600 | tf_op jit(solution)/shard_map/reshape | solution.py:450
  54.6 1.7 %copy.39 = bf16[2,12,8,40,80]{4,2,3,1,0:T(8,128)(2,1)} copy(bf16[2,12,8,40,80]{4,3,2,1,0:T(8,128)(2,1)S(1)} %reshape.64) | data formatting | bytes 2457600 | tf_op jit(solution)/shard_map/reshape | solution.py:450
  56.3 3.2 %reshape.65.canvas = bf16[2,480,640]{2,1,0:T(8,128)(2,1)S(1)} reshape(bf16[2,12,40,8,80]{4,3,2,1,0:T(8,128)(2,1)} %bitcast.8) | data formatting | bytes 2457600 | tf_op jit(solution)/shard_map/reshape | solution.py:452
  59.6 0.0 copy-start
  59.6 0.0 copy-start.1
  59.6 0.0 copy-start.2
  59.6 0.0 copy-start.3
  59.6 0.0 copy-start.4
  59.6 0.0 copy-start.6
  59.6 14.2 %shard_map.140.images = bf16[2,608,896]{2,1,0:T(8,128)(2,1)S(1)} custom-call(bf16[2,480,640]{2,1,0:T(8,128)(2,1)S(1)} %reshape.65.canvas), custom_call_target="tpu_custom_call" | custom-call | tf_op jit(solution)/shard_map/pallas_call | solution.py:311
  73.8 0.0 copy-done
  73.8 0.0 copy-done.1
  73.8 0.0 copy-done.2
  73.9 0.0 copy-done.3
  73.9 0.0 copy-done.4
  73.9 0.0 copy-done.6
  73.9 37.3 %shard_map.141 = (f32[2,12,16]{2,1,0:T(8,128)S(1)}, f32[12,16]{1,0:T(8,128)S(1)}) custom-call(bf16[2,608,896]{2,1,0:T(8,128)(2,1)S(1)} %shard_map.140.images, bf16[2,416,256]{2,1,0:T(8,128)(2,1)S(1)} %copy-done.1, bf16[352,208]{1,0:T(8,128)(2,1)S(1)} %copy-done.2, bf16[160,176]{1,0:T(8,128)(2,1)S(1)} %copy-done.4, bf16[256,256]{1,0:T(8,128)(2,1)S(1)} %copy-done.3, ...), custom_call_target="tpu_custom_call" | custom-call | tf_op jit(solution)/shard_map/pallas_call | solution.py:208
  111.2 0.0 copy-start.7
  111.2 0.6 copy-done.7
  111.8 0.0 copy-start.5
  111.8 0.6 copy.34
  112.4 0.0 copy-done.5
  112.5 10.7 %shard_map.142 = f32[2,12,16]{2,1,0:T(8,128)} custom-call(f32[2,12,16]{2,1,0:T(8,128)} %copy-done.5, f32[12,16]{1,0:T(8,128)} %copy-done.7, s32[12,16]{1,0:T(8,128)} %valid.1), custom_call_target="tpu_custom_call" | custom-call | tf_op jit(solution)/shard_map/pallas_call | solution.py:398
  123.1 1.3 %copy.35 = f32[2,12,16]{2,0,1:T(2,128)} copy(f32[2,12,16]{2,1,0:T(8,128)} %shard_map.142) | data formatting | bytes 3072
  (1 shorter events, 0.0 us)
Async XLA Ops:
  59.6 14.3 %copy-start = (f32[896,128]{1,0:T(8,128)S(1)}, f32[896,128]{1,0:T(8,128)}, u32[]{:S(2)}) copy-start(f32[896,128]{1,0:T(8,128)} %constant.81.clone.band_cols) | copy-start | bytes 1376260
  59.6 14.3 %copy-start.1 = (bf16[2,416,256]{2,1,0:T(8,128)(2,1)S(1)}, bf16[2,416,256]{2,1,0:T(8,128)(2,1)}, u32[]{:S(2)}) copy-start(bf16[2,416,256]{2,1,0:T(8,128)(2,1)} %constant.76.clone.first) | copy-start | bytes 1277956
  59.6 14.3 %copy-start.2 = (bf16[352,208]{1,0:T(8,128)(2,1)S(1)}, bf16[352,208]{1,0:T(8,128)(2,1)}, u32[]{:S(2)}) copy-start(bf16[352,208]{1,0:T(8,128)(2,1)} %constant.77.clone.second) | copy-start | bytes 439300
  59.6 14.3 %copy-start.3 = (bf16[256,256]{1,0:T(8,128)(2,1)S(1)}, bf16[256,256]{1,0:T(8,128)(2,1)}, u32[]{:S(2)}) copy-start(bf16[256,256]{1,0:T(8,128)(2,1)} %constant.79.clone.fourth) | copy-start | bytes 393220
  59.6 14.3 %copy-start.4 = (bf16[160,176]{1,0:T(8,128)(2,1)S(1)}, bf16[160,176]{1,0:T(8,128)(2,1)}, u32[]{:S(2)}) copy-start(bf16[160,176]{1,0:T(8,128)(2,1)} %constant.78.clone.third) | copy-start | bytes 168964
  59.6 14.2 %copy-start.6 = (bf16[16,608]{1,0:T(8,128)(2,1)S(1)}, bf16[16,608]{1,0:T(8,128)(2,1)}, u32[]{:S(2)}) copy-start(bf16[16,608]{1,0:T(8,128)(2,1)} %constant.80.clone.band_rows) | copy-start | bytes 58372
  111.2 0.6 copy-start.7
  111.8 0.6 copy-start.5

commit v4 on v3

--- a/solution.py
+++ b/solution.py
@@ -1,3 +1,4 @@
+import functools
 import math
 
 import jax
@@ -410,42 +411,143 @@
     )(flow, sure, valid)
 
 
-def slots(tile_owner):
-    index = jnp.arange(tile_owner.shape[0], dtype=jnp.int32)
-    earlier = (tile_owner[:, None] == tile_owner[None, :]) & (index[:, None] > index[None, :])
-    return tile_owner, jnp.sum(earlier.astype(jnp.int32), axis=1)
+MSG_ROWS = 16
+CUT = 1536
+MSG_COLS = 1664
+
+
+def route_kernel(
+    a_tiles, b_tiles, owners, offsets, out, send, recv, code_rows, send_sem, recv_sem,
+    *, capacity, tile_h, tile_w,
+):
+    row, col = lax.axis_index("row"), lax.axis_index("col")
+    col_count = lax.axis_size("col")
+    devices = lax.axis_size("row") * col_count
+    me = row * col_count + col
+    tile_count = a_tiles.shape[0]
+    chunk = 128 // MSG_ROWS
+    barrier = pltpu.get_barrier_semaphore()
+
+    def device(k):
+        target = lax.rem(me + k, devices)
+        return (lax.div(target, col_count), lax.rem(target, col_count))
+
+    def greet(k, carry):
+        pl.semaphore_signal(barrier, inc=1, device_id=device(k), device_id_type=MESH)
+        return carry
+
+    lax.fori_loop(1, devices, greet, 0)
+
+    def copy(k):
+        return pltpu.make_async_remote_copy(
+            src_ref=send.at[k],
+            dst_ref=recv.at[k],
+            send_sem=send_sem.at[k],
+            recv_sem=recv_sem.at[k],
+            device_id=device(k),
+            device_id_type=MESH,
+        )
+
+    earlier = lax.broadcasted_iota(jnp.int32, (tile_count, tile_count), 0)
+    later = lax.broadcasted_iota(jnp.int32, (tile_count, tile_count), 1)
+    targets, places = [], []
+    for section in range(2):
+        across = owners[section : section + 1, :].astype(jnp.float32)
+        down = jnp.sum(jnp.where(earlier == later, across, 0.0), axis=1, keepdims=True)
+        same = (down == across) & (earlier < later)
+        rank = jnp.sum(jnp.where(same, 1.0, 0.0), axis=0, keepdims=True)
+        ahead = across - me.astype(jnp.float32)
+        ahead = jnp.where(ahead < 0.0, ahead + devices, ahead)
+        targets.append(ahead * MSG_ROWS + rank + section * capacity)
+        at = offsets[2 * section : 2 * section + 2, :].astype(jnp.float32)
+        place_y = jnp.floor(at[0:1] * (1.0 / tile_h) + 0.5)
+        place_x = jnp.floor(at[1:2] * (1.0 / tile_w) + 0.5)
+        places.append(place_y * TX + place_x + 1.0)
+    slot = lax.broadcasted_iota(jnp.int32, (128, tile_count), 0)
+
+    def fill(c, carry):
+        here = (slot + c * 128).astype(jnp.float32)
+        code = jnp.zeros((128, 1), jnp.float32)
+        left = jnp.zeros((128, CUT), jnp.float32)
+        right = jnp.zeros((128, MSG_COLS - CUT), jnp.float32)
+        for tiles, target, place in zip((a_tiles, b_tiles), targets, places):
+            upper = jnp.where(here == target, 1.0, 0.0)
+            lower = jnp.where(here == target + 8.0, 1.0, 0.0).astype(jnp.bfloat16)
+            code = code + jnp.sum(upper * place, axis=1, keepdims=True)
+            left = left + dot(upper.astype(jnp.bfloat16), tiles[:, :CUT])
+            left = left + dot(lower, tiles[:, CUT : 2 * CUT])
+            right = right + dot(lower, tiles[:, 2 * CUT :])
+        block = pl.ds(c * chunk, chunk)
+        send[block, :, :CUT] = left.astype(jnp.bfloat16).reshape(chunk, MSG_ROWS, CUT)
+        send[block, :, CUT:] = (
+            (right + code).astype(jnp.bfloat16).reshape(chunk, MSG_ROWS, MSG_COLS - CUT)
+        )
+
+        @pl.when(c == 0)
+        def _():
+            pl.semaphore_wait(barrier, devices - 1)
+            recv[0] = send[0]
+
+        def push(k, carry):
+            copy(k).start()
+            return carry
+
+        lax.fori_loop(jnp.maximum(c * chunk, 1), (c + 1) * chunk, push, 0)
+        return carry
+
+    lax.fori_loop(0, devices // chunk, fill, 0)
+
+    def arrive(k, carry):
+        copy(k).wait()
+        return carry
+
+    lax.fori_loop(1, devices, arrive, 0)
+
+    from_row = lax.broadcasted_iota(jnp.int32, (128, 128), 0)
+    to_lane = lax.broadcasted_iota(jnp.int32, (128, 128), 1)
+    to_lane = jnp.where((to_lane & 15) >= 8, to_lane - 8, to_lane)
+    for c in range(devices // chunk):
+        codes = recv[c * chunk : (c + 1) * chunk, :, CUT:].reshape(128, 128).astype(jnp.float32)
+        code_rows[:, 128 * c : 128 * (c + 1)] = jnp.sum(
+            jnp.where(from_row == to_lane, codes[:, :1], 0.0), axis=0, keepdims=True
+        )
+    shape = (2 * tile_count, devices * MSG_ROWS)
+    wanted = lax.broadcasted_iota(jnp.int32, shape, 0).astype(jnp.float32) + 1.0
+    within = lax.broadcasted_iota(jnp.int32, (1, shape[1]), 1) & 15
+    code = code_rows[...]
+    code = jnp.where((within & 7) >= capacity, code + tile_count, code)
+    code = jnp.where(code_rows[...] > 0.0, code, 0.0)
+    for half, (start, size) in enumerate(((0, CUT), (CUT, MSG_COLS))):
+        in_half = (within >= 8) if half else (within < 8)
+        select = jnp.where(wanted == jnp.where(in_half, code, 0.0), 1.0, 0.0).astype(jnp.bfloat16)
+        rows = recv[:, :, :size].reshape(shape[1], size)
+        out[:, start : start + size] = dot(select, rows).astype(jnp.bfloat16)
 
 
 def routed(tiles, owners, offsets, devices, capacity, tile_h, tile_w):
     tile_count, tile_size = tiles[0].shape
-    targets, rows = [], []
-    for section in range(2):
-        owner, rank = slots(owners[section])
-        targets.append(owner * (2 * capacity) + section * capacity + rank)
-        offset = offsets[section]
-        place = offset[:, 0] // tile_h * TX + offset[:, 1] // tile_w + 1
-        code = jnp.pad(place.astype(jnp.bfloat16)[:, None], ((0, 0), (0, 127)))
-        rows.append(jnp.concatenate([tiles[section], code], axis=1))
-    target = jnp.concatenate(targets)
-    slot = jnp.arange(devices * 2 * capacity, dtype=jnp.int32)
-    select = (slot[:, None] == target[None, :]).astype(jnp.bfloat16)
-    sent = jnp.dot(
-        select, jnp.concatenate(rows, axis=0), preferred_element_type=jnp.float32
-    ).astype(jnp.bfloat16)
-    got = lax.all_to_all(
-        sent.reshape(devices, 2 * capacity, tile_size + 128),
-        ("row", "col"),
-        split_axis=0,
-        concat_axis=0,
-        tiled=True,
-    ).reshape(devices * 2 * capacity, tile_size + 128)
-    came = slot // capacity % 2 * tile_count + got[:, tile_size].astype(jnp.int32) - 1
-    came = jnp.where(got[:, tile_size] > 0, came, -1)
-    wanted = jnp.arange(2 * tile_count, dtype=jnp.int32)
-    select = (came[None, :] == wanted[:, None]).astype(jnp.bfloat16)
-    blocks = jnp.dot(
-        select, got[:, :tile_size], preferred_element_type=jnp.float32
-    ).astype(jnp.bfloat16)
+    vmem = pl.BlockSpec(memory_space=pltpu.VMEM)
+    buffer = pltpu.VMEM((devices, MSG_ROWS, MSG_COLS), jnp.bfloat16)
+    blocks = pl.pallas_call(
+        functools.partial(route_kernel, capacity=capacity, tile_h=tile_h, tile_w=tile_w),
+        out_shape=jax.ShapeDtypeStruct((2 * tile_count, tile_size), jnp.bfloat16),
+        in_specs=[vmem] * 4,
+        out_specs=vmem,
+        scratch_shapes=[
+            buffer,
+            buffer,
+            pltpu.VMEM((1, devices * MSG_ROWS), jnp.float32),
+            pltpu.SemaphoreType.DMA((devices,)),
+            pltpu.SemaphoreType.DMA((devices,)),
+        ],
+        compiler_params=pltpu.CompilerParams(
+            collective_id=2, has_side_effects=True, vmem_limit_bytes=40 * 1024 * 1024
+        ),
+    )(
+        *tiles,
+        jnp.stack(owners),
+        jnp.concatenate([offset.T for offset in offsets], axis=0),
+    )
     return (
         blocks.reshape(2, TY, TX, tile_h, tile_w)
         .transpose(0, 1, 3, 2, 4)

time: 125 us -> 121 us (0.968)
  blocking collectives: 44.8 us -> 0 us
  Pallas kernels: 62.2 us -> 105 us
  local copies, waits for them, and re-layouts: 9.95 us -> 13.2 us
  other arithmetic: 4.38 us -> 1.38 us
  matrix products: 2.36 us -> 0 us
    all_to_all x1 -> x0, blocking collectives: 44.8 us -> none  [routed(): lax.all_to_all(sent.reshape(devices, 2 * capacity, tile_size + 128), ('ro...]
    pallas_call x0 -> x1, Pallas kernels: none -> 43.4 us  [routed(): pl.pallas_call(functools.partial(route_kernel, capacity=capacity, tile_h=...]
    unnamed x20 -> x22, local copies, waits for them, and re-layouts: 2.85 us -> 6.06 us
    dot_general x2 -> x0, matrix products: 2.36 us -> none  [the longest x1 1.86 us: routed(): jnp.dot(select, jnp.concatenate(rows, axis=0), preferred_element_type=jnp...]
    reduce_sum x2 -> x0, other arithmetic: 1.83 us -> none  [slots(): return (tile_owner, jnp.sum(earlier.astype(jnp.int32), axis=1))]
    convert_element_type x3 -> x0, other arithmetic: 1.66 us -> none  [the longest x2 1.54 us: routed(): code = jnp.pad(place.astype(jnp.bfloat16)[:, None], ((0, 0), (0, 127)))]
where the time goes in v4:
time: 121 us; the launch traced here: 120 us
  Pallas kernels  105 us (87%)
  local copies, waits for them, and re-layouts  13.2 us (11%)
  other arithmetic  1.38 us (1%)
    pallas_call x1, Pallas kernels, routed(): pl.pallas_call(functools.partial(route_kernel, capacity=capacity, tile_h=...  43.4 us
    pallas_call x1, Pallas kernels, correlate(): pl.pallas_call(correlate_kernel, out_shape=(jax.ShapeDtypeStruct((2, grid...  37.3 us
    pallas_call x1, Pallas kernels, with_halo(): pl.pallas_call(halo_kernel, out_shape=jax.ShapeDtypeStruct((2, ROWS, COLS...  13.5 us
    pallas_call x1, Pallas kernels, relaxed(): pl.pallas_call(mesh_kernel, out_shape=jax.ShapeDtypeStruct(flow.shape, jn...  10.8 us
    unnamed x22, local copies, waits for them, and re-layouts  6.06 us
    reshape x2, local copies, waits for them, and re-layouts, routed(): blocks.reshape(2, TY, TX, tile_h, tile_w).transpose(0, 1, 3, 2, 4)  3.88 us
    reshape x1, local copies, waits for them, and re-layouts, routed(): return blocks.reshape(2, TY, TX, tile_h, tile_w).transpose(0, 1, 3, 2, 4)...  3.24 us

profile of v4, /device:TPU:13, one launch (start us, length us, event | category | flops | bytes accessed | tf_op | source)
XLA Modules:
  0.0 120.3 jit_solution(5917199914943976534)
XLA Ops:
  0.6 0.7 pad_add_fusion.1.owners
  1.3 0.7 pad_add_fusion.offsets
  2.0 0.0 copy-start
  2.0 1.1 copy-done
  3.1 0.0 copy-start.1
  3.1 1.1 copy-done.1
  4.2 43.4 %shard_map.140 = bf16[192,3200]{1,0:T(8,128)(2,1)S(1)} custom-call(bf16[96,3200]{1,0:T(8,128)(2,1)S(1)} %copy-done, bf16[96,3200]{1,0:T(8,128)(2,1)S(1)} %copy-done.1, s32[2,96]{1,0:T(2,128)S(1)} %pad_add_fusion.1.owners, s32[4,96]{1,0:T(4,128)S(1)} %pad_add_fusion.offsets), custom_call_target="tpu_custom_call" | custom-call | tf_op jit(solution)/shard_map/pallas_call | solution.py:531
  47.6 2.2 %reshape.10 = bf16[2,12,8,40,80]{4,3,2,1,0:T(8,128)(2,1)S(1)} reshape(bf16[192,3200]{1,0:T(8,128)(2,1)S(1)} %shard_map.140) | data formatting | bytes 2457600 | tf_op jit(solution)/shard_map/reshape | solution.py:552
  49.7 1.7 %copy.19 = bf16[2,12,8,40,80]{4,2,3,1,0:T(8,128)(2,1)} copy(bf16[2,12,8,40,80]{4,3,2,1,0:T(8,128)(2,1)S(1)} %reshape.10) | data formatting | bytes 2457600 | tf_op jit(solution)/shard_map/reshape | solution.py:552
  51.4 3.2 %reshape.11.canvas = bf16[2,480,640]{2,1,0:T(8,128)(2,1)S(1)} reshape(bf16[2,12,40,8,80]{4,3,2,1,0:T(8,128)(2,1)} %bitcast.9) | data formatting | bytes 2457600 | tf_op jit(solution)/shard_map/reshape | solution.py:554
  54.7 0.0 copy-start.2
  54.7 0.0 copy-start.3
  54.7 0.0 copy-start.4
  54.7 0.0 copy-start.5
  54.7 0.0 copy-start.6
  54.8 0.0 copy-start.8
  54.8 13.5 %shard_map.141.images = bf16[2,608,896]{2,1,0:T(8,128)(2,1)S(1)} custom-call(bf16[2,480,640]{2,1,0:T(8,128)(2,1)S(1)} %reshape.11.canvas), custom_call_target="tpu_custom_call" | custom-call | tf_op jit(solution)/shard_map/pallas_call | solution.py:312
  68.3 0.0 copy-done.2
  68.3 0.0 copy-done.3
  68.3 0.0 copy-done.4
  68.3 0.0 copy-done.5
  68.3 0.0 copy-done.6
  68.3 0.0 copy-done.8
  68.4 37.3 %shard_map.142 = (f32[2,12,16]{2,1,0:T(8,128)S(1)}, f32[12,16]{1,0:T(8,128)S(1)}) custom-call(bf16[2,608,896]{2,1,0:T(8,128)(2,1)S(1)} %shard_map.141.images, bf16[2,416,256]{2,1,0:T(8,128)(2,1)S(1)} %copy-done.3, bf16[352,208]{1,0:T(8,128)(2,1)S(1)} %copy-done.4, bf16[160,176]{1,0:T(8,128)(2,1)S(1)} %copy-done.6, bf16[256,256]{1,0:T(8,128)(2,1)S(1)} %copy-done.5, ...), custom_call_target="tpu_custom_call" | custom-call | tf_op jit(solution)/shard_map/pallas_call | solution.py:209
  105.7 0.0 copy-start.7
  105.7 0.6 copy-done.7
  106.3 0.0 copy-start.9
  106.3 0.6 copy-done.9
  106.9 10.8 %shard_map.143 = f32[2,12,16]{2,1,0:T(8,128)} custom-call(f32[2,12,16]{2,1,0:T(8,128)} %copy-done.7, f32[12,16]{1,0:T(8,128)} %copy-done.9, s32[12,16]{1,0:T(8,128)} %valid.1), custom_call_target="tpu_custom_call" | custom-call | tf_op jit(solution)/shard_map/pallas_call | solution.py:399
  117.7 1.3 %copy.16 = f32[2,12,16]{2,0,1:T(2,128)} copy(f32[2,12,16]{2,1,0:T(8,128)} %copy-done.7) | data formatting | bytes 3072
  119.0 1.3 %copy.17 = f32[2,12,16]{2,0,1:T(2,128)} copy(f32[2,12,16]{2,1,0:T(8,128)} %shard_map.143) | data formatting | bytes 3072
Async XLA Ops:
  2.0 1.1 copy-start
  3.1 1.1 copy-start.1
  54.7 13.6 %copy-start.2 = (f32[896,128]{1,0:T(8,128)S(1)}, f32[896,128]{1,0:T(8,128)}, u32[]{:S(2)}) copy-start(f32[896,128]{1,0:T(8,128)} %constant.17.clone.band_cols) | copy-start | bytes 1376260
  54.7 13.6 %copy-start.3 = (bf16[2,416,256]{2,1,0:T(8,128)(2,1)S(1)}, bf16[2,416,256]{2,1,0:T(8,128)(2,1)}, u32[]{:S(2)}) copy-start(bf16[2,416,256]{2,1,0:T(8,128)(2,1)} %constant.12.clone.first) | copy-start | bytes 1277956
  54.7 13.6 %copy-start.4 = (bf16[352,208]{1,0:T(8,128)(2,1)S(1)}, bf16[352,208]{1,0:T(8,128)(2,1)}, u32[]{:S(2)}) copy-start(bf16[352,208]{1,0:T(8,128)(2,1)} %constant.13.clone.second) | copy-start | bytes 439300
  54.7 13.6 %copy-start.5 = (bf16[256,256]{1,0:T(8,128)(2,1)S(1)}, bf16[256,256]{1,0:T(8,128)(2,1)}, u32[]{:S(2)}) copy-start(bf16[256,256]{1,0:T(8,128)(2,1)} %constant.15.clone.fourth) | copy-start | bytes 393220
  54.7 13.6 %copy-start.6 = (bf16[160,176]{1,0:T(8,128)(2,1)S(1)}, bf16[160,176]{1,0:T(8,128)(2,1)}, u32[]{:S(2)}) copy-start(bf16[160,176]{1,0:T(8,128)(2,1)} %constant.14.clone.third) | copy-start | bytes 168964
  54.8 13.6 %copy-start.8 = (bf16[16,608]{1,0:T(8,128)(2,1)S(1)}, bf16[16,608]{1,0:T(8,128)(2,1)}, u32[]{:S(2)}) copy-start(bf16[16,608]{1,0:T(8,128)(2,1)} %constant.16.clone.band_rows) | copy-start | bytes 58372
  105.7 0.6 copy-start.7
  106.3 0.6 copy-start.9

commit v5 on v4

--- a/solution.py
+++ b/solution.py
@@ -75,29 +75,51 @@
     return jnp.dot(left, right, preferred_element_type=jnp.float32)
 
 
-def correlate_kernel(
-    images, first, second, third, fourth, band_rows, band_cols, flow, sure, spec, scale, parts,
-    spectra_0, spectra_1, inverse_0, inverse_1,
+def section_kernel(
+    canvas, valid, first, second, third, fourth, band_rows, band_cols, flow, mesh,
+    images, spec, scale, parts, spectra_0, spectra_1, inverse_0, inverse_1,
+    sure, mine, near, send_sem, recv_sem,
 ):
-    grid_rows, grid_cols = sure.shape
-    half_rows = ROWS // 2
-
-    def first_part(step, carry):
-        section = step // 2
-        top = pl.multiple_of(step % 2 * half_rows, 16)
-        for j in range(grid_cols):
+    row, col = lax.axis_index("row"), lax.axis_index("col")
+    grid_rows, grid_cols = valid.shape
+    height, width = canvas.shape[1:]
+    near[...] = jnp.zeros(near.shape, jnp.float32)
+    copies = halo_copies(canvas, images, row, col, send_sem, recv_sem)
+    greet_neighbours(row, col)
+    start(row, col, copies)
+    images[:, EDGE_R : EDGE_R + height, EDGE_C : EDGE_C + width] = canvas[...]
+
+    def first_part(source, section, top, count, from_lane, to_row, columns):
+        for j in columns:
             left = (COL0 + STRIDE * j) // 128 * 128
             inside = COL0 + STRIDE * j - left
             width = 256 if inside + PATCH <= 256 else 384
             parity = inside // 8 % 2
             base = 132 + 8 * parity - inside
-            strip = images[section, pl.ds(top, half_rows), left : left + width]
-            spec[section, pl.ds(top, half_rows), 256 * j : 256 * (j + 1)] = dot(
+            strip = source[section, top : top + count, left - from_lane : left - from_lane + width]
+            spec[section, to_row : to_row + count, 256 * j : 256 * (j + 1)] = dot(
                 strip, first[parity, base : base + width, :]
             ).astype(jnp.bfloat16)
+
+    half = height // 2
+    inner = [j for j in range(2, grid_cols - 2)]
+    outer = [j for j in range(grid_cols) if j not in inner]
+
+    def first_inner(section, carry):
+        for top in (0, half):
+            first_part(canvas, section, top, half, EDGE_C, EDGE_R + top, inner)
         return carry
 
-    lax.fori_loop(0, 4, first_part, 0)
+    def first_outer(section, carry):
+        for top in (EDGE_R, EDGE_R + half):
+            first_part(images, section, top, half, 0, top, outer)
+        for top in (0, EDGE_R + height):
+            first_part(images, section, top, EDGE_R, 0, top, range(grid_cols))
+        return carry
+
+    lax.fori_loop(0, 2, first_inner, 0)
+    finish(row, col, copies)
+    lax.fori_loop(0, 2, first_outer, 0)
 
     norms = []
     for section in range(2):
@@ -202,19 +224,20 @@
         sure[i : i + 1, :] = sums[0] / below
         flow[0, i : i + 1, :] = sums[1] / below
         flow[1, i : i + 1, :] = sums[2] / below
-
-
-def correlate(images, grid_rows, grid_cols):
+    relax(flow, sure, valid, mesh, mine, near, send_sem, recv_sem)
+
+
+def measured(canvas, valid):
+    grid_rows, grid_cols = valid.shape
     vmem = pl.BlockSpec(memory_space=pltpu.VMEM)
+    field = jax.ShapeDtypeStruct((2, grid_rows, grid_cols), jnp.float32)
     return pl.pallas_call(
-        correlate_kernel,
-        out_shape=(
-            jax.ShapeDtypeStruct((2, grid_rows, grid_cols), jnp.float32),
-            jax.ShapeDtypeStruct((grid_rows, grid_cols), jnp.float32),
-        ),
-        in_specs=[vmem] * 7,
+        section_kernel,
+        out_shape=(field, field),
+        in_specs=[vmem] * 8,
         out_specs=(vmem, vmem),
         scratch_shapes=[
+            pltpu.VMEM((2, ROWS, COLS), jnp.bfloat16),
             pltpu.VMEM((2, ROWS, 256 * grid_cols), jnp.bfloat16),
             pltpu.VMEM((16, 128), jnp.float32),
             pltpu.VMEM((3, 2, grid_rows // 2 * grid_cols + 8, 128), jnp.float32),
@@ -222,9 +245,16 @@
             pltpu.VMEM((2, 4 * KPAD, 256), jnp.float32),
             pltpu.VMEM((2 * PATCH, 256), jnp.bfloat16),
             pltpu.VMEM((2 * PATCH, 256), jnp.bfloat16),
+            pltpu.VMEM((grid_rows, grid_cols), jnp.float32),
+            pltpu.VMEM((3, 24, 128), jnp.float32),
+            pltpu.VMEM((8, 3, 24, 128), jnp.float32),
+            pltpu.SemaphoreType.DMA((16,)),
+            pltpu.SemaphoreType.DMA((16,)),
         ],
-        compiler_params=pltpu.CompilerParams(vmem_limit_bytes=48 * 1024 * 1024),
-    )(images, *tables())
+        compiler_params=pltpu.CompilerParams(
+            collective_id=0, has_side_effects=True, vmem_limit_bytes=48 * 1024 * 1024
+        ),
+    )(canvas, valid, *tables())
 
 
 DIRECTIONS = [(dr, dc) for dr in (-1, 0, 1) for dc in (-1, 0, 1) if (dr, dc) != (0, 0)]
@@ -255,13 +285,15 @@
     pl.semaphore_wait(barrier, along(row, "row") * along(col, "col") - 1)
 
 
-def exchange(row, col, copies):
+def start(row, col, copies):
     for (dr, dc), copy in zip(DIRECTIONS, copies):
 
         @pl.when(exists(row + dr, col + dc))
         def _(copy=copy):
             copy.start()
 
+
+def finish(row, col, copies):
     for (dr, dc), copy in zip(DIRECTIONS, copies):
 
         @pl.when(exists(row + dr, col + dc))
@@ -273,15 +305,13 @@
             copy.wait_recv()
 
 
-def halo_kernel(canvas, image, send_sem, recv_sem):
-    row, col = lax.axis_index("row"), lax.axis_index("col")
+def halo_copies(canvas, image, row, col, send_sem, recv_sem):
     height, width = canvas.shape[1:]
     image[:, :EDGE_R, :] = jnp.zeros((2, EDGE_R, COLS), jnp.bfloat16)
     image[:, EDGE_R + height :, :] = jnp.zeros((2, EDGE_R, COLS), jnp.bfloat16)
     side = jnp.zeros((2, height, EDGE_C), jnp.bfloat16)
     image[:, EDGE_R : EDGE_R + height, :EDGE_C] = side
     image[:, EDGE_R : EDGE_R + height, EDGE_C + width :] = side
-    greet_neighbours(row, col)
     rows = {
         -1: (slice(0, EDGE_R), slice(EDGE_R + height, ROWS)),
         0: (slice(0, height), slice(EDGE_R, EDGE_R + height)),
@@ -292,7 +322,7 @@
         0: (slice(0, width), slice(EDGE_C, EDGE_C + width)),
         1: (slice(width - EDGE_C, width), slice(0, EDGE_C)),
     }
-    copies = [
+    return [
         pltpu.make_async_remote_copy(
             src_ref=canvas.at[:, rows[dr][0], cols[dc][0]],
             dst_ref=image.at[:, rows[dr][1], cols[dc][1]],
@@ -303,46 +333,29 @@
         )
         for d, (dr, dc) in enumerate(DIRECTIONS)
     ]
-    image[:, EDGE_R : EDGE_R + height, EDGE_C : EDGE_C + width] = canvas[...]
-    exchange(row, col, copies)
-
-
-def with_halo(canvas):
-    vmem = pl.BlockSpec(memory_space=pltpu.VMEM)
-    return pl.pallas_call(
-        halo_kernel,
-        out_shape=jax.ShapeDtypeStruct((2, ROWS, COLS), jnp.bfloat16),
-        in_specs=[vmem],
-        out_specs=vmem,
-        scratch_shapes=[pltpu.SemaphoreType.DMA((8,)), pltpu.SemaphoreType.DMA((8,))],
-        compiler_params=pltpu.CompilerParams(
-            collective_id=0, has_side_effects=True, vmem_limit_bytes=32 * 1024 * 1024
-        ),
-    )(canvas)
-
-
-def mesh_kernel(flow, sure, valid, out, mine, near, send_sem, recv_sem):
+
+
+def relax(flow, sure, valid, out, mine, near, send_sem, recv_sem):
     row, col = lax.axis_index("row"), lax.axis_index("col")
     grid_rows, grid_cols = valid.shape
-    near[...] = jnp.zeros(near.shape, jnp.float32)
     mine[...] = jnp.zeros(mine.shape, jnp.float32)
     usable = valid[...].astype(jnp.float32)
     mine[0, :grid_rows, :grid_cols] = usable * sure[...]
     mine[1, :grid_rows, :grid_cols] = usable * flow[0]
     mine[2, :grid_rows, :grid_cols] = usable * flow[1]
-    greet_neighbours(row, col)
     copies = [
         pltpu.make_async_remote_copy(
             src_ref=mine,
             dst_ref=near.at[d],
-            send_sem=send_sem.at[d],
-            recv_sem=recv_sem.at[d],
+            send_sem=send_sem.at[8 + d],
+            recv_sem=recv_sem.at[8 + d],
             device_id=(row + dr, col + dc),
             device_id_type=MESH,
         )
         for d, (dr, dc) in enumerate(DIRECTIONS)
     ]
-    exchange(row, col, copies)
+    start(row, col, copies)
+    finish(row, col, copies)
     shape = mine.shape[1:]
     i = lax.broadcasted_iota(jnp.int32, shape, 0)
     j = lax.broadcasted_iota(jnp.int32, shape, 1)
@@ -383,9 +396,9 @@
         & (i < grid_rows + 2 * SWEEPS)
         & (j < grid_cols + 2 * SWEEPS)
     )
-    for f, start in enumerate((start_y, start_x)):
-        pull = strength * start
-        field = start
+    for f, initial in enumerate((start_y, start_x)):
+        pull = strength * initial
+        field = initial
         for _ in range(SWEEPS):
             around = moved(field, 1, 0) + moved(field, -1, 0)
             around = around + moved(field, 0, 1) + moved(field, 0, -1)
@@ -394,30 +407,13 @@
         out[f] = moved(field, -SWEEPS, -SWEEPS)[:grid_rows, :grid_cols]
 
 
-def relaxed(flow, sure, valid):
-    vmem = pl.BlockSpec(memory_space=pltpu.VMEM)
-    return pl.pallas_call(
-        mesh_kernel,
-        out_shape=jax.ShapeDtypeStruct(flow.shape, jnp.float32),
-        in_specs=[vmem] * 3,
-        out_specs=vmem,
-        scratch_shapes=[
-            pltpu.VMEM((3, 24, 128), jnp.float32),
-            pltpu.VMEM((8, 3, 24, 128), jnp.float32),
-            pltpu.SemaphoreType.DMA((8,)),
-            pltpu.SemaphoreType.DMA((8,)),
-        ],
-        compiler_params=pltpu.CompilerParams(collective_id=1, has_side_effects=True),
-    )(flow, sure, valid)
-
-
 MSG_ROWS = 16
 CUT = 1536
 MSG_COLS = 1664
 
 
 def route_kernel(
-    a_tiles, b_tiles, owners, offsets, out, send, recv, code_rows, send_sem, recv_sem,
+    a_tiles, b_tiles, a_owner, b_owner, a_offset, b_offset, out, send, recv, code_rows, send_sem, recv_sem,
     *, capacity, tile_h, tile_w,
 ):
     row, col = lax.axis_index("row"), lax.axis_index("col")
@@ -451,15 +447,15 @@
     earlier = lax.broadcasted_iota(jnp.int32, (tile_count, tile_count), 0)
     later = lax.broadcasted_iota(jnp.int32, (tile_count, tile_count), 1)
     targets, places = [], []
-    for section in range(2):
-        across = owners[section : section + 1, :].astype(jnp.float32)
+    for section, (owner, offset) in enumerate(((a_owner, a_offset), (b_owner, b_offset))):
+        across = owner[...].astype(jnp.float32)
         down = jnp.sum(jnp.where(earlier == later, across, 0.0), axis=1, keepdims=True)
         same = (down == across) & (earlier < later)
         rank = jnp.sum(jnp.where(same, 1.0, 0.0), axis=0, keepdims=True)
         ahead = across - me.astype(jnp.float32)
         ahead = jnp.where(ahead < 0.0, ahead + devices, ahead)
         targets.append(ahead * MSG_ROWS + rank + section * capacity)
-        at = offsets[2 * section : 2 * section + 2, :].astype(jnp.float32)
+        at = offset[...].astype(jnp.float32)
         place_y = jnp.floor(at[0:1] * (1.0 / tile_h) + 0.5)
         place_x = jnp.floor(at[1:2] * (1.0 / tile_w) + 0.5)
         places.append(place_y * TX + place_x + 1.0)
@@ -531,7 +527,7 @@
     blocks = pl.pallas_call(
         functools.partial(route_kernel, capacity=capacity, tile_h=tile_h, tile_w=tile_w),
         out_shape=jax.ShapeDtypeStruct((2 * tile_count, tile_size), jnp.bfloat16),
-        in_specs=[vmem] * 4,
+        in_specs=[vmem] * 6,
         out_specs=vmem,
         scratch_shapes=[
             buffer,
@@ -545,8 +541,8 @@
         ),
     )(
         *tiles,
-        jnp.stack(owners),
-        jnp.concatenate([offset.T for offset in offsets], axis=0),
+        *(owner.reshape(1, tile_count) for owner in owners),
+        *(offset.T for offset in offsets),
     )
     return (
         blocks.reshape(2, TY, TX, tile_h, tile_w)
@@ -570,8 +566,7 @@
         tile_h,
         tile_w,
     )
-    flow_field, confidence = correlate(with_halo(canvas), grid_rows, grid_cols)
-    return flow_field, relaxed(flow_field, confidence, patch_valid)
+    return measured(canvas, patch_valid)
 
 
 def solution(mesh):

time: 121 us -> 113 us (0.934)
  Pallas kernels: 105 us -> 97.3 us
  other arithmetic: 1.38 us -> 0 us
    pallas_call x3 -> x1, Pallas kernels: 61.6 us -> 54 us  [measured(): pl.pallas_call(section_kernel, out_shape=(field, field), in_specs=[vmem]...]
    unnamed x22 -> x26, local copies, waits for them, and re-layouts: 6.06 us -> 4.84 us
    pallas_call x0 -> x2, local copies, waits for them, and re-layouts: none -> 1.21 us  [measured(): pl.pallas_call(section_kernel, out_shape=(field, field), in_specs=[vmem]...]
where the time goes in v5:
time: 113 us; the launch traced here: 111 us
  Pallas kernels  97.3 us (86%)
  local copies, waits for them, and re-layouts  13.3 us (12%)
    pallas_call x1, Pallas kernels, measured(): pl.pallas_call(section_kernel, out_shape=(field, field), in_specs=[vmem]...  54 us
    pallas_call x1, Pallas kernels, routed(): pl.pallas_call(functools.partial(route_kernel, capacity=capacity, tile_h=...  43.4 us
    unnamed x26, local copies, waits for them, and re-layouts  4.84 us
    reshape x2, local copies, waits for them, and re-layouts, routed(): blocks.reshape(2, TY, TX, tile_h, tile_w).transpose(0, 1, 3, 2, 4)  3.88 us
    reshape x1, local copies, waits for them, and re-layouts, routed(): return blocks.reshape(2, TY, TX, tile_h, tile_w).transpose(0, 1, 3, 2, 4)...  3.34 us

profile of v5, /device:TPU:13, one launch (start us, length us, event | category | flops | bytes accessed | tf_op | source)
XLA Modules:
  0.0 111.4 jit_solution(8524839892735957248)
XLA Ops:
  0.6 0.0 copy-start
  0.6 1.1 copy-done
  1.7 0.0 copy-start.1
  1.7 1.1 copy-done.1
  2.8 0.0 copy-start.9
  2.8 0.7 copy-done.9
  3.5 0.0 copy-start.10
  3.5 0.7 copy-done.10
  4.1 0.0 copy-start.11
  4.1 0.7 copy-done.11
  4.8 0.0 copy-start.12
  4.8 0.7 copy-done.12
  5.5 43.4 %shard_map.140 = bf16[192,3200]{1,0:T(8,128)(2,1)S(1)} custom-call(bf16[96,3200]{1,0:T(8,128)(2,1)S(1)} %copy-done, bf16[96,3200]{1,0:T(8,128)(2,1)S(1)} %copy-done.1, s32[1,96]{1,0:T(1,128)S(1)} %bitcast.11, s32[1,96]{1,0:T(1,128)S(1)} %bitcast.12, s32[2,96]{1,0:T(2,128)S(1)} %bitcast.9, s32[2,96]{1,0:T(2,128)S(1)} %bitcast.10), custom_call_target="tpu_custom_call" | custom-call | tf_op jit(solution)/shard_map/pallas_call | solution.py:527
  48.8 2.2 %reshape.18 = bf16[2,12,8,40,80]{4,3,2,1,0:T(8,128)(2,1)S(1)} reshape(bf16[192,3200]{1,0:T(8,128)(2,1)S(1)} %shard_map.140) | data formatting | bytes 2457600 | tf_op jit(solution)/shard_map/reshape | solution.py:548
  51.0 1.7 %copy.19 = bf16[2,12,8,40,80]{4,2,3,1,0:T(8,128)(2,1)} copy(bf16[2,12,8,40,80]{4,3,2,1,0:T(8,128)(2,1)S(1)} %reshape.18) | data formatting | bytes 2457600 | tf_op jit(solution)/shard_map/reshape | solution.py:548
  52.7 0.0 copy-start.2
  52.7 0.0 copy-start.3
  52.7 0.0 copy-start.4
  52.7 0.0 copy-start.5
  52.7 0.0 copy-start.6
  52.8 0.0 copy-start.7
  52.8 0.0 copy-start.8
  52.8 3.3 %reshape.19.canvas = bf16[2,480,640]{2,1,0:T(8,128)(2,1)S(1)} reshape(bf16[2,12,40,8,80]{4,3,2,1,0:T(8,128)(2,1)} %bitcast.13) | data formatting | bytes 2457600 | tf_op jit(solution)/shard_map/reshape | solution.py:550
  56.1 0.0 copy-done.2
  56.1 0.0 copy-done.3
  56.2 0.0 copy-done.4
  56.2 0.0 copy-done.5
  56.2 0.0 copy-done.6
  56.2 0.0 copy-done.7
  56.2 0.0 copy-done.8
  56.2 54.0 %shard_map.141 = (f32[2,12,16]{2,1,0:T(8,128)S(1)}, f32[2,12,16]{2,1,0:T(8,128)S(1)}) custom-call(bf16[2,480,640]{2,1,0:T(8,128)(2,1)S(1)} %reshape.19.canvas, s32[12,16]{1,0:T(8,128)S(1)} %copy-done.8, bf16[2,416,256]{2,1,0:T(8,128)(2,1)S(1)} %copy-done.3, bf16[352,208]{1,0:T(8,128)(2,1)S(1)} %copy-done.4, bf16[160,176]{1,0:T(8,128)(2,1)S(1)} %copy-done.6, ...), custom_call_target="tpu_custom_call" | custom-call | tf_op jit(solution)/shard_map/pallas_call | solution.py:234
  110.2 0.6 copy.16
  110.8 0.6 copy.17
Async XLA Ops:
  0.6 1.1 copy-start
  1.7 1.1 copy-start.1
  2.8 0.7 copy-start.9
  3.5 0.7 copy-start.10
  4.1 0.7 copy-start.11
  4.8 0.7 copy-start.12
  52.7 3.4 %copy-start.2 = (f32[896,128]{1,0:T(8,128)S(1)}, f32[896,128]{1,0:T(8,128)}, u32[]{:S(2)}) copy-start(f32[896,128]{1,0:T(8,128)} %constant.17.clone.band_cols) | copy-start | bytes 1376260
  52.7 3.4 %copy-start.3 = (bf16[2,416,256]{2,1,0:T(8,128)(2,1)S(1)}, bf16[2,416,256]{2,1,0:T(8,128)(2,1)}, u32[]{:S(2)}) copy-start(bf16[2,416,256]{2,1,0:T(8,128)(2,1)} %constant.12.clone.first) | copy-start | bytes 1277956
  52.7 3.4 %copy-start.4 = (bf16[352,208]{1,0:T(8,128)(2,1)S(1)}, bf16[352,208]{1,0:T(8,128)(2,1)}, u32[]{:S(2)}) copy-start(bf16[352,208]{1,0:T(8,128)(2,1)} %constant.13.clone.second) | copy-start | bytes 439300
  52.7 3.4 %copy-start.5 = (bf16[256,256]{1,0:T(8,128)(2,1)S(1)}, bf16[256,256]{1,0:T(8,128)(2,1)}, u32[]{:S(2)}) copy-start(bf16[256,256]{1,0:T(8,128)(2,1)} %constant.15.clone.fourth) | copy-start | bytes 393220
  52.7 3.4 %copy-start.6 = (bf16[160,176]{1,0:T(8,128)(2,1)S(1)}, bf16[160,176]{1,0:T(8,128)(2,1)}, u32[]{:S(2)}) copy-start(bf16[160,176]{1,0:T(8,128)(2,1)} %constant.14.clone.third) | copy-start | bytes 168964
  52.8 3.4 %copy-start.7 = (bf16[16,608]{1,0:T(8,128)(2,1)S(1)}, bf16[16,608]{1,0:T(8,128)(2,1)}, u32[]{:S(2)}) copy-start(bf16[16,608]{1,0:T(8,128)(2,1)} %constant.16.clone.band_rows) | copy-start | bytes 58372
  52.8 3.4 %copy-start.8 = (s32[12,16]{1,0:T(8,128)S(1)}, s32[12,16]{1,0:T(8,128)}, u32[]{:S(2)}) copy-start(s32[12,16]{1,0:T(8,128)} %valid.1) | copy-start | bytes 2308

commit v6 on v5

--- a/solution.py
+++ b/solution.py
@@ -76,28 +76,33 @@
 
 
 def section_kernel(
-    canvas, valid, first, second, third, fourth, band_rows, band_cols, flow, mesh,
+    strips, valid, first, second, third, fourth, band_rows, band_cols, flow, mesh,
     images, spec, scale, parts, spectra_0, spectra_1, inverse_0, inverse_1,
     sure, mine, near, send_sem, recv_sem,
 ):
     row, col = lax.axis_index("row"), lax.axis_index("col")
     grid_rows, grid_cols = valid.shape
-    height, width = canvas.shape[1:]
+    _, strip_count, height, strip_width = strips.shape
+    width = strip_count * strip_width
     near[...] = jnp.zeros(near.shape, jnp.float32)
-    copies = halo_copies(canvas, images, row, col, send_sem, recv_sem)
+    copies = halo_copies(images, height, width, row, col, send_sem, recv_sem)
     greet_neighbours(row, col)
+    for section in range(2):
+        for n in range(strip_count):
+            left = EDGE_C + n * strip_width
+            images[section, EDGE_R : EDGE_R + height, left : left + strip_width] = strips[section, n]
+    await_neighbours(row, col)
     start(row, col, copies)
-    images[:, EDGE_R : EDGE_R + height, EDGE_C : EDGE_C + width] = canvas[...]
-
-    def first_part(source, section, top, count, from_lane, to_row, columns):
+
+    def first_part(section, top, count, columns):
         for j in columns:
             left = (COL0 + STRIDE * j) // 128 * 128
             inside = COL0 + STRIDE * j - left
             width = 256 if inside + PATCH <= 256 else 384
             parity = inside // 8 % 2
             base = 132 + 8 * parity - inside
-            strip = source[section, top : top + count, left - from_lane : left - from_lane + width]
-            spec[section, to_row : to_row + count, 256 * j : 256 * (j + 1)] = dot(
+            strip = images[section, top : top + count, left : left + width]
+            spec[section, top : top + count, 256 * j : 256 * (j + 1)] = dot(
                 strip, first[parity, base : base + width, :]
             ).astype(jnp.bfloat16)
 
@@ -106,15 +111,15 @@
     outer = [j for j in range(grid_cols) if j not in inner]
 
     def first_inner(section, carry):
-        for top in (0, half):
-            first_part(canvas, section, top, half, EDGE_C, EDGE_R + top, inner)
+        for top in (EDGE_R, EDGE_R + half):
+            first_part(section, top, half, inner)
         return carry
 
     def first_outer(section, carry):
         for top in (EDGE_R, EDGE_R + half):
-            first_part(images, section, top, half, 0, top, outer)
+            first_part(section, top, half, outer)
         for top in (0, EDGE_R + height):
-            first_part(images, section, top, EDGE_R, 0, top, range(grid_cols))
+            first_part(section, top, EDGE_R, range(grid_cols))
         return carry
 
     lax.fori_loop(0, 2, first_inner, 0)
@@ -227,7 +232,7 @@
     relax(flow, sure, valid, mesh, mine, near, send_sem, recv_sem)
 
 
-def measured(canvas, valid):
+def measured(strips, valid):
     grid_rows, grid_cols = valid.shape
     vmem = pl.BlockSpec(memory_space=pltpu.VMEM)
     field = jax.ShapeDtypeStruct((2, grid_rows, grid_cols), jnp.float32)
@@ -254,7 +259,7 @@
         compiler_params=pltpu.CompilerParams(
             collective_id=0, has_side_effects=True, vmem_limit_bytes=48 * 1024 * 1024
         ),
-    )(canvas, valid, *tables())
+    )(strips, valid, *tables())
 
 
 DIRECTIONS = [(dr, dc) for dr in (-1, 0, 1) for dc in (-1, 0, 1) if (dr, dc) != (0, 0)]
@@ -279,10 +284,12 @@
                 barrier, inc=1, device_id=(row + dr, col + dc), device_id_type=MESH
             )
 
+
+def await_neighbours(row, col):
     def along(index, axis):
         return 1 + jnp.where(index > 0, 1, 0) + jnp.where(index < lax.axis_size(axis) - 1, 1, 0)
 
-    pl.semaphore_wait(barrier, along(row, "row") * along(col, "col") - 1)
+    pl.semaphore_wait(pltpu.get_barrier_semaphore(), along(row, "row") * along(col, "col") - 1)
 
 
 def start(row, col, copies):
@@ -305,26 +312,25 @@
             copy.wait_recv()
 
 
-def halo_copies(canvas, image, row, col, send_sem, recv_sem):
-    height, width = canvas.shape[1:]
+def halo_copies(image, height, width, row, col, send_sem, recv_sem):
     image[:, :EDGE_R, :] = jnp.zeros((2, EDGE_R, COLS), jnp.bfloat16)
     image[:, EDGE_R + height :, :] = jnp.zeros((2, EDGE_R, COLS), jnp.bfloat16)
     side = jnp.zeros((2, height, EDGE_C), jnp.bfloat16)
     image[:, EDGE_R : EDGE_R + height, :EDGE_C] = side
     image[:, EDGE_R : EDGE_R + height, EDGE_C + width :] = side
     rows = {
-        -1: (slice(0, EDGE_R), slice(EDGE_R + height, ROWS)),
-        0: (slice(0, height), slice(EDGE_R, EDGE_R + height)),
-        1: (slice(height - EDGE_R, height), slice(0, EDGE_R)),
+        -1: (slice(EDGE_R, 2 * EDGE_R), slice(EDGE_R + height, ROWS)),
+        0: (slice(EDGE_R, EDGE_R + height), slice(EDGE_R, EDGE_R + height)),
+        1: (slice(height, EDGE_R + height), slice(0, EDGE_R)),
     }
     cols = {
-        -1: (slice(0, EDGE_C), slice(EDGE_C + width, COLS)),
-        0: (slice(0, width), slice(EDGE_C, EDGE_C + width)),
-        1: (slice(width - EDGE_C, width), slice(0, EDGE_C)),
+        -1: (slice(EDGE_C, 2 * EDGE_C), slice(EDGE_C + width, COLS)),
+        0: (slice(EDGE_C, EDGE_C + width), slice(EDGE_C, EDGE_C + width)),
+        1: (slice(width, EDGE_C + width), slice(0, EDGE_C)),
     }
     return [
         pltpu.make_async_remote_copy(
-            src_ref=canvas.at[:, rows[dr][0], cols[dc][0]],
+            src_ref=image.at[:, rows[dr][0], cols[dc][0]],
             dst_ref=image.at[:, rows[dr][1], cols[dc][1]],
             send_sem=send_sem.at[d],
             recv_sem=recv_sem.at[d],
@@ -413,9 +419,25 @@
 
 
 def route_kernel(
-    a_tiles, b_tiles, a_owner, b_owner, a_offset, b_offset, out, send, recv, code_rows, send_sem, recv_sem,
+    a_hbm, b_hbm, a_owner_hbm, b_owner_hbm, a_offset_hbm, b_offset_hbm, out, send, recv, code_rows, send_sem, recv_sem,
+    a_tiles, b_tiles, a_owner, b_owner, a_offset, b_offset, load_sem,
     *, capacity, tile_h, tile_w,
 ):
+    loads = [
+        pltpu.make_async_copy(source, target, load_sem.at[n])
+        for n, (source, target) in enumerate(
+            (
+                (a_owner_hbm, a_owner),
+                (b_owner_hbm, b_owner),
+                (a_offset_hbm, a_offset),
+                (b_offset_hbm, b_offset),
+                (a_hbm, a_tiles),
+                (b_hbm, b_tiles),
+            )
+        )
+    ]
+    for load in loads:
+        load.start()
     row, col = lax.axis_index("row"), lax.axis_index("col")
     col_count = lax.axis_size("col")
     devices = lax.axis_size("row") * col_count
@@ -444,6 +466,8 @@
             device_id_type=MESH,
         )
 
+    for load in loads[:4]:
+        load.wait()
     earlier = lax.broadcasted_iota(jnp.int32, (tile_count, tile_count), 0)
     later = lax.broadcasted_iota(jnp.int32, (tile_count, tile_count), 1)
     targets, places = [], []
@@ -460,6 +484,8 @@
         place_x = jnp.floor(at[1:2] * (1.0 / tile_w) + 0.5)
         places.append(place_y * TX + place_x + 1.0)
     slot = lax.broadcasted_iota(jnp.int32, (128, tile_count), 0)
+    for load in loads[4:]:
+        load.wait()
 
     def fill(c, carry):
         here = (slot + c * 128).astype(jnp.float32)
@@ -527,7 +553,7 @@
     blocks = pl.pallas_call(
         functools.partial(route_kernel, capacity=capacity, tile_h=tile_h, tile_w=tile_w),
         out_shape=jax.ShapeDtypeStruct((2 * tile_count, tile_size), jnp.bfloat16),
-        in_specs=[vmem] * 6,
+        in_specs=[pl.BlockSpec(memory_space=pltpu.HBM)] * 6,
         out_specs=vmem,
         scratch_shapes=[
             buffer,
@@ -535,9 +561,13 @@
             pltpu.VMEM((1, devices * MSG_ROWS), jnp.float32),
             pltpu.SemaphoreType.DMA((devices,)),
             pltpu.SemaphoreType.DMA((devices,)),
+            *[pltpu.VMEM((tile_count, tile_size), jnp.bfloat16)] * 2,
+            *[pltpu.VMEM((1, tile_count), jnp.int32)] * 2,
+            *[pltpu.VMEM((2, tile_count), jnp.int32)] * 2,
+            pltpu.SemaphoreType.DMA((6,)),
         ],
         compiler_params=pltpu.CompilerParams(
-            collective_id=2, has_side_effects=True, vmem_limit_bytes=40 * 1024 * 1024
+            collective_id=2, has_side_effects=True, vmem_limit_bytes=63 * 1024 * 1024
         ),
     )(
         *tiles,
@@ -546,8 +576,8 @@
     )
     return (
         blocks.reshape(2, TY, TX, tile_h, tile_w)
-        .transpose(0, 1, 3, 2, 4)
-        .reshape(2, TY * tile_h, TX * tile_w)
+        .transpose(0, 2, 1, 3, 4)
+        .reshape(2, TX, TY * tile_h, tile_w)
     )
 
 
@@ -557,7 +587,7 @@
     tile_w = grid_cols * STRIDE // TX
     devices = lax.axis_size("row") * lax.axis_size("col")
     capacity = 4 * a_tiles.shape[0] // (3 * devices)
-    canvas = routed(
+    strips = routed(
         (a_tiles, b_tiles),
         (a_owner, b_owner),
         (a_offset, b_offset),
@@ -566,7 +596,7 @@
         tile_h,
         tile_w,
     )
-    return measured(canvas, patch_valid)
+    return measured(strips, patch_valid)
 
 
 def solution(mesh):

time: 113 us -> 107 us (0.947)
  local copies, waits for them, and re-layouts: 13.3 us -> 5.81 us
  Pallas kernels: 97.3 us -> 98.9 us
    unnamed x26 -> x14, local copies, waits for them, and re-layouts: 4.84 us -> 0.86 us
    reshape x3 -> x2, local copies, waits for them, and re-layouts: 7.22 us -> 3.74 us  [routed(): blocks.reshape(2, TY, TX, tile_h, tile_w).transpose(0, 2, 1, 3, 4)]
    pallas_call x1, Pallas kernels: 43.4 us -> 44.7 us  [routed(): pl.pallas_call(functools.partial(route_kernel, capacity=capacity, tile_h=...]
where the time goes in v6:
time: 107 us; the launch traced here: 105 us
  Pallas kernels  98.9 us (92%)
  local copies, waits for them, and re-layouts  5.81 us (5%)
    pallas_call x1, Pallas kernels, measured(): pl.pallas_call(section_kernel, out_shape=(field, field), in_specs=[vmem]...  54.2 us
    pallas_call x1, Pallas kernels, routed(): pl.pallas_call(functools.partial(route_kernel, capacity=capacity, tile_h=...  44.7 us
    reshape x2, local copies, waits for them, and re-layouts, routed(): blocks.reshape(2, TY, TX, tile_h, tile_w).transpose(0, 2, 1, 3, 4)  3.74 us

profile of v6, /device:TPU:13, one launch (start us, length us, event | category | flops | bytes accessed | tf_op | source)
XLA Modules:
  0.0 105.5 jit_solution(7006185372962643754)
XLA Ops:
  0.6 44.7 %shard_map.140 = bf16[192,3200]{1,0:T(8,128)(2,1)} custom-call(bf16[96,3200]{1,0:T(8,128)(2,1)} %a_hbm.1, bf16[96,3200]{1,0:T(8,128)(2,1)} %b_hbm.1, s32[1,96]{1,0:T(1,128)} %bitcast.10, s32[1,96]{1,0:T(1,128)} %bitcast.11, s32[2,96]{1,0:T(2,128)} %bitcast.8, s32[2,96]{1,0:T(2,128)} %bitcast.9), custom_call_target="tpu_custom_call" | custom-call | tf_op jit(solution)/shard_map/pallas_call | solution.py:553
  45.4 3.4 %reshape.18 = bf16[2,12,8,40,80]{4,3,2,1,0:T(8,128)(2,1)S(1)} reshape(bf16[192,3200]{1,0:T(8,128)(2,1)} %shard_map.140) | data formatting | bytes 2457600 | tf_op jit(solution)/shard_map/reshape | solution.py:578
  48.8 0.0 copy-start
  48.8 0.0 copy-start.1
  48.8 0.0 copy-start.2
  48.8 0.0 copy-start.3
  48.8 0.0 copy-start.4
  48.8 0.0 copy-start.5
  48.8 0.0 copy-start.6
  48.9 0.3 copy.15
  49.2 0.6 copy-done
  49.8 0.1 copy-done.1
  49.9 0.0 copy-done.2
  50.0 0.0 copy-done.3
  50.0 0.0 copy-done.4
  50.0 0.0 copy-done.5
  50.0 0.0 copy-done.6
  50.0 54.2 %shard_map.141 = (f32[2,12,16]{2,1,0:T(8,128)S(1)}, f32[2,12,16]{2,1,0:T(8,128)S(1)}) custom-call(bf16[2,8,480,80]{3,2,1,0:T(8,128)(2,1)S(1)} %bitcast.7, s32[12,16]{1,0:T(8,128)S(1)} %copy-done.6, bf16[2,416,256]{2,1,0:T(8,128)(2,1)S(1)} %copy-done.1, bf16[352,208]{1,0:T(8,128)(2,1)S(1)} %copy-done.2, bf16[160,176]{1,0:T(8,128)(2,1)S(1)} %copy-done.4, ...), custom_call_target="tpu_custom_call" | custom-call | tf_op jit(solution)/shard_map/pallas_call | solution.py:239
  104.2 0.6 copy.16
  104.9 0.6 copy.17
Async XLA Ops:
  48.8 1.0 copy-start
  48.8 1.1 %copy-start.1 = (bf16[2,416,256]{2,1,0:T(8,128)(2,1)S(1)}, bf16[2,416,256]{2,1,0:T(8,128)(2,1)}, u32[]{:S(2)}) copy-start(bf16[2,416,256]{2,1,0:T(8,128)(2,1)} %constant.12.clone.first) | copy-start | bytes 1277956
  48.8 1.2 %copy-start.2 = (bf16[352,208]{1,0:T(8,128)(2,1)S(1)}, bf16[352,208]{1,0:T(8,128)(2,1)}, u32[]{:S(2)}) copy-start(bf16[352,208]{1,0:T(8,128)(2,1)} %constant.13.clone.second) | copy-start | bytes 439300
  48.8 1.2 %copy-start.3 = (bf16[256,256]{1,0:T(8,128)(2,1)S(1)}, bf16[256,256]{1,0:T(8,128)(2,1)}, u32[]{:S(2)}) copy-start(bf16[256,256]{1,0:T(8,128)(2,1)} %constant.15.clone.fourth) | copy-start | bytes 393220
  48.8 1.2 %copy-start.4 = (bf16[160,176]{1,0:T(8,128)(2,1)S(1)}, bf16[160,176]{1,0:T(8,128)(2,1)}, u32[]{:S(2)}) copy-start(bf16[160,176]{1,0:T(8,128)(2,1)} %constant.14.clone.third) | copy-start | bytes 168964
  48.8 1.2 %copy-start.5 = (bf16[16,608]{1,0:T(8,128)(2,1)S(1)}, bf16[16,608]{1,0:T(8,128)(2,1)}, u32[]{:S(2)}) copy-start(bf16[16,608]{1,0:T(8,128)(2,1)} %constant.16.clone.band_rows) | copy-start | bytes 58372
  48.8 1.2 %copy-start.6 = (s32[12,16]{1,0:T(8,128)S(1)}, s32[12,16]{1,0:T(8,128)}, u32[]{:S(2)}) copy-start(s32[12,16]{1,0:T(8,128)} %valid.1) | copy-start | bytes 2308

commit v7 on v6

--- a/solution.py
+++ b/solution.py
@@ -208,7 +208,7 @@
         forward(t + 2, spectra_0)
         return carry
 
-    lax.fori_loop(0, pairs // 2, step, 0)
+    lax.fori_loop(0, pairs // 2, step, 0, unroll=2)
     summed(pairs - 1, inverse_1)
 
     ones = jnp.ones((8, 128), jnp.float32)

time: 107 us -> 107 us (level)
  no operation moved by 1% of the time
where the time goes in v7:
time: 107 us; the launch traced here: 105 us
  Pallas kernels  98.1 us (92%)
  local copies, waits for them, and re-layouts  5.81 us (5%)
    pallas_call x1, Pallas kernels, measured(): pl.pallas_call(section_kernel, out_shape=(field, field), in_specs=[vmem]...  53.4 us
    pallas_call x1, Pallas kernels, routed(): pl.pallas_call(functools.partial(route_kernel, capacity=capacity, tile_h=...  44.7 us
    reshape x2, local copies, waits for them, and re-layouts, routed(): blocks.reshape(2, TY, TX, tile_h, tile_w).transpose(0, 2, 1, 3, 4)  3.74 us

profile of v7, /device:TPU:13, one launch (start us, length us, event | category | flops | bytes accessed | tf_op | source)
XLA Modules:
  0.0 104.7 jit_solution(3002750540091893181)
XLA Ops:
  0.6 44.7 %shard_map.140 = bf16[192,3200]{1,0:T(8,128)(2,1)} custom-call(bf16[96,3200]{1,0:T(8,128)(2,1)} %a_hbm.1, bf16[96,3200]{1,0:T(8,128)(2,1)} %b_hbm.1, s32[1,96]{1,0:T(1,128)} %bitcast.10, s32[1,96]{1,0:T(1,128)} %bitcast.11, s32[2,96]{1,0:T(2,128)} %bitcast.8, s32[2,96]{1,0:T(2,128)} %bitcast.9), custom_call_target="tpu_custom_call" | custom-call | tf_op jit(solution)/shard_map/pallas_call | solution.py:553
  45.4 3.4 %reshape.18 = bf16[2,12,8,40,80]{4,3,2,1,0:T(8,128)(2,1)S(1)} reshape(bf16[192,3200]{1,0:T(8,128)(2,1)} %shard_map.140) | data formatting | bytes 2457600 | tf_op jit(solution)/shard_map/reshape | solution.py:578
  48.8 0.0 copy-start
  48.8 0.0 copy-start.1
  48.8 0.0 copy-start.2
  48.8 0.0 copy-start.3
  48.8 0.0 copy-start.4
  48.8 0.0 copy-start.5
  48.8 0.0 copy-start.6
  48.9 0.3 copy.15
  49.2 0.6 copy-done
  49.8 0.1 copy-done.1
  49.9 0.0 copy-done.2
  50.0 0.0 copy-done.3
  50.0 0.0 copy-done.4
  50.0 0.0 copy-done.5
  50.0 0.0 copy-done.6
  50.0 53.4 %shard_map.141 = (f32[2,12,16]{2,1,0:T(8,128)S(1)}, f32[2,12,16]{2,1,0:T(8,128)S(1)}) custom-call(bf16[2,8,480,80]{3,2,1,0:T(8,128)(2,1)S(1)} %bitcast.7, s32[12,16]{1,0:T(8,128)S(1)} %copy-done.6, bf16[2,416,256]{2,1,0:T(8,128)(2,1)S(1)} %copy-done.1, bf16[352,208]{1,0:T(8,128)(2,1)S(1)} %copy-done.2, bf16[160,176]{1,0:T(8,128)(2,1)S(1)} %copy-done.4, ...), custom_call_target="tpu_custom_call" | custom-call | tf_op jit(solution)/shard_map/pallas_call | solution.py:239
  103.5 0.6 copy.16
  104.1 0.6 copy.17
Async XLA Ops:
  48.8 1.0 copy-start
  48.8 1.1 %copy-start.1 = (bf16[2,416,256]{2,1,0:T(8,128)(2,1)S(1)}, bf16[2,416,256]{2,1,0:T(8,128)(2,1)}, u32[]{:S(2)}) copy-start(bf16[2,416,256]{2,1,0:T(8,128)(2,1)} %constant.12.clone.first) | copy-start | bytes 1277956
  48.8 1.2 %copy-start.2 = (bf16[352,208]{1,0:T(8,128)(2,1)S(1)}, bf16[352,208]{1,0:T(8,128)(2,1)}, u32[]{:S(2)}) copy-start(bf16[352,208]{1,0:T(8,128)(2,1)} %constant.13.clone.second) | copy-start | bytes 439300
  48.8 1.2 %copy-start.3 = (bf16[256,256]{1,0:T(8,128)(2,1)S(1)}, bf16[256,256]{1,0:T(8,128)(2,1)}, u32[]{:S(2)}) copy-start(bf16[256,256]{1,0:T(8,128)(2,1)} %constant.15.clone.fourth) | copy-start | bytes 393220
  48.8 1.2 %copy-start.4 = (bf16[160,176]{1,0:T(8,128)(2,1)S(1)}, bf16[160,176]{1,0:T(8,128)(2,1)}, u32[]{:S(2)}) copy-start(bf16[160,176]{1,0:T(8,128)(2,1)} %constant.14.clone.third) | copy-start | bytes 168964
  48.8 1.2 %copy-start.5 = (bf16[16,608]{1,0:T(8,128)(2,1)S(1)}, bf16[16,608]{1,0:T(8,128)(2,1)}, u32[]{:S(2)}) copy-start(bf16[16,608]{1,0:T(8,128)(2,1)} %constant.16.clone.band_rows) | copy-start | bytes 58372
  48.8 1.2 %copy-start.6 = (s32[12,16]{1,0:T(8,128)S(1)}, s32[12,16]{1,0:T(8,128)}, u32[]{:S(2)}) copy-start(s32[12,16]{1,0:T(8,128)} %valid.1) | copy-start | bytes 2308
